TPU v7x, 256 devices: a whole 4x4x8 slice. The times are simulated.
256 devices in a mesh: vis: 64 (over z, x, core), head: 4 (over y).
Axes of the slice: x: 4, y: 4, z: 8, core: 2. Of those that a mesh axis runs over, the one named last changes fastest.
Arguments:
- patches: bfloat16 [24576, 1280], P('vis'), may hold values from -6 to 6
- norm_gain: float32 [1280], replicated, may hold values from 0.4 to 1.6
- w_qkv: bfloat16 [1280, 3, 1280], P(None, None, 'head'), may hold values from -1 to 1
- w_out: bfloat16 [1280, 1280], P(None, 'head'), may hold values from -0.15625 to 0.15625
- grad_y: bfloat16 [24576, 1280], P('vis'), may hold values from -16 to 16
- window_ids: int32 [24576], replicated, may hold values from 0 to 511, never falling along the last dimension, each value on 1 to 64 neighbouring positions
Outputs:
- grad_x: bfloat16 [24576, 1280], P('vis', 'head')
- grad_qkv: float32 [1280, 3, 1280], P('vis', None, 'head')
- grad_out: float32 [1280, 1280], P('vis', 'head')
- grad_gain: float32 [1280], P('head')
Inputs may be any that keep to these rules, and one draw needn't show every extreme that they name: `window_ids`: window numbers never fall along the patches, and each window holds 1 to 64 patches, one exactly 64.
All inputs are finite; a program needn't handle non-finite values.
Results may differ from a plain program's by a relative error of at most 0.03.
Values may be sent and summed in bfloat16 or wider, within the bound.
A program may use at most 64 MiB of HBM per device.

v0:
```python
import jax
import jax.numpy as jnp
from jax import lax
from jax.sharding import PartitionSpec as P

HEAD_DIM = 80
WIN = 64


norm_epsilon = 1e-06


def extended_2(block, sides, width):
    for axis, dim in sides:
        count = lax.axis_size(axis)
        forward = [(i, i + 1) for i in range(count - 1)]
        backward = [(target, source) for source, target in forward]
        low = lax.ppermute(
            lax.slice_in_dim(block, block.shape[dim] - width, None, axis=dim), axis, forward
        )
        high = lax.ppermute(lax.slice_in_dim(block, 0, width, axis=dim), axis, backward)
        block = jnp.concatenate([low, block, high], axis=dim)
    return block


def from_behind(block, axis, distance):
    devices = range(lax.axis_size(axis))
    route = [(i - distance, i) for i in devices if i - distance in devices]
    return lax.ppermute(block, axis, route)


def attention_grads(query, keyval, own_ids, key_ids, grad_att):
    f32 = jnp.float32
    row_count = query.shape[0]
    key_span = keyval.shape[0]
    heads = query.shape[1] // HEAD_DIM
    scale = HEAD_DIM ** (-0.5)
    q_heads = query.reshape(row_count, heads, HEAD_DIM)
    k_heads = keyval[:, 0].reshape(key_span, heads, HEAD_DIM)
    v_heads = keyval[:, 1].reshape(key_span, heads, HEAD_DIM)
    g_heads = grad_att.reshape(row_count, heads, HEAD_DIM)
    scores = jnp.einsum("rhe,khe->hrk", q_heads, k_heads, preferred_element_type=f32) * scale
    same_window = own_ids[:, None] == key_ids[None, :]
    scores = jnp.where(same_window[None], scores, -1e30)
    highest = jnp.max(scores, axis=2, keepdims=True)
    weights = jnp.exp(scores - highest)
    weights = weights / jnp.sum(weights, axis=2, keepdims=True)
    probs = weights.astype(jnp.bfloat16)
    attended = jnp.einsum("hrk,khe->rhe", probs, v_heads, preferred_element_type=f32).astype(
        jnp.bfloat16
    )
    delta = jnp.sum(attended.astype(f32) * g_heads.astype(f32), axis=2)
    dprob = jnp.einsum("rhe,khe->hrk", g_heads, v_heads, preferred_element_type=f32)
    dscore = (weights * (dprob - jnp.transpose(delta)[:, :, None]) * scale).astype(jnp.bfloat16)
    grad_q = jnp.einsum("hrk,khe->rhe", dscore, k_heads, preferred_element_type=f32).astype(
        jnp.bfloat16
    )
    grad_k = jnp.einsum("hrk,rhe->khe", dscore, q_heads, preferred_element_type=f32)
    grad_v = jnp.einsum("hrk,rhe->khe", probs, g_heads, preferred_element_type=f32)
    key_grads = jnp.stack([grad_k.reshape(key_span, -1), grad_v.reshape(key_span, -1)], axis=1)
    return (attended.reshape(row_count, -1), grad_q.reshape(row_count, -1), key_grads)


def per_device(patches, norm_gain, w_qkv, w_out, grad_y, window_ids):
    f32 = jnp.float32
    bf16 = jnp.bfloat16
    row_count, feature_count = patches.shape
    vis_index = lax.axis_index("vis")
    head_index = lax.axis_index("head")
    share_width = feature_count // lax.axis_size("head")
    inputs = patches.astype(f32)
    inverse = lax.rsqrt(jnp.mean(inputs * inputs, axis=1, keepdims=True) + norm_epsilon)
    normed = (inputs * inverse * norm_gain[None, :]).astype(bf16)
    project = jnp.einsum("rd,dcj->rcj", normed, w_qkv, preferred_element_type=f32).astype(bf16)
    keyval = project[:, 1:]
    extended = extended_2(keyval, (("vis", 0),), WIN)
    padded_ids = jnp.pad(window_ids, (WIN, WIN), constant_values=-1)
    first_row = vis_index * row_count
    own_ids = lax.dynamic_slice_in_dim(window_ids, first_row, row_count, 0)
    key_ids = lax.dynamic_slice_in_dim(padded_ids, first_row, row_count + 2 * WIN, 0)
    grad_att = jnp.dot(grad_y, w_out, preferred_element_type=f32).astype(bf16)
    attended, grad_q, key_grads = attention_grads(
        project[:, 0], extended, own_ids, key_ids, grad_att
    )
    center = key_grads[WIN : WIN + row_count]
    from_below = from_behind(key_grads[:WIN].astype(jnp.bfloat16), "vis", -1).astype(jnp.float32)
    from_above = from_behind(key_grads[WIN + row_count :].astype(jnp.bfloat16), "vis", 1).astype(
        jnp.float32
    )
    center = center.at[row_count - WIN :].add(from_below)
    center = center.at[:WIN].add(from_above)
    grad_proj = jnp.concatenate([grad_q[:, None, :], center.astype(bf16)], axis=1)
    partial_normed = jnp.einsum("rcj,dcj->rd", grad_proj, w_qkv, preferred_element_type=f32)
    share_start = head_index * share_width
    grad_normed = lax.psum(partial_normed.astype(jnp.bfloat16), "head").astype(jnp.float32)
    scaled = grad_normed * norm_gain[None, :]
    product_mean = jnp.mean(scaled * inputs, axis=1, keepdims=True)
    full_x = grad_y.astype(f32) + inverse * (scaled - inputs * inverse * inverse * product_mean)
    grad_x = lax.dynamic_slice_in_dim(full_x, share_start, share_width, 1).astype(bf16)
    gain_full = jnp.sum(grad_normed * inputs * inverse, axis=0)
    gain_part = lax.dynamic_slice_in_dim(gain_full, share_start, share_width, 0)
    grad_gain = lax.psum(gain_part, "vis")
    qkv_local = jnp.einsum("rd,rcj->dcj", normed, grad_proj, preferred_element_type=f32)
    out_local = jnp.einsum("ro,ri->oi", grad_y, attended, preferred_element_type=f32)
    grad_qkv, grad_out = (
        lax.psum_scatter(qkv_local, "vis", scatter_dimension=0, tiled=True),
        lax.psum_scatter(out_local, "vis", scatter_dimension=0, tiled=True),
    )
    return (grad_x, grad_qkv, grad_out, grad_gain)


def solution(mesh):
    in_specs = (P("vis", None), P(), P(None, None, "head"), P(None, "head"), P("vis", None), P())
    out_specs = (P("vis", "head"), P("vis", None, "head"), P("vis", "head"), P("head"))
    return jax.shard_map(
        per_device, mesh=mesh, in_specs=in_specs, out_specs=out_specs, check_vma=False
    )
```

profile of v0, /device:TPU:1, one launch (start us, length us, event | category | flops | bytes accessed | tf_op | source)
XLA Modules:
  0.0 332.7 jit_solution(15508720095110121392)
XLA Ops:
  7.2 0.0 copy-start
  7.2 0.0 all-reduce.7.cloned.1.call-start
  7.2 1.6 fusion.3
  8.9 0.3 copy-done
  9.2 2.8 convolution_convert_fusion
  12.0 0.0 copy-done.11
  12.0 0.0 copy-start.7
  12.0 0.9 copy-done.7
  12.9 0.8 fusion.29
  13.7 4.5 %collective-permute-start = (bf16[64,2,320]{0,2,1:T(8,128)(2,1)}, bf16[64,2,320]{0,2,1:T(8,128)(2,1)}, u32[]{:S(2)}, u32[]{:S(2)}) collective-permute-start(bf16[64,2,320]{0,2,1:T(8,128)(2,1)} %get-tuple-element.42), channel_id=1, source_target_pairs={{0,4},{4,8},{8,12},{12,16},{16,20},{20,24},{24,28},{28,32},{32,36}... | collective-permute-start | bytes 245768 | tf_op jit(solution)/shard_map/ppermute | solution.py:18
  18.2 2.6 collective-permute-start.1
  20.8 0.0 copy-done.10
  20.8 0.0 copy-start.8
  20.8 0.1 pad_dynamic-slice_fusion
  20.9 0.1 dynamic_slice.12
  21.0 0.0 copy-done.6
  21.0 2.5 convolution_convert_fusion.3
  23.5 0.2 broadcast_compare_fusion
  23.7 0.0 copy-done.8
  23.7 0.1 slice.92
  23.8 0.0 collective-permute-done
  23.8 1.4 collective-permute-done.1
  25.1 1.3 pad_maximum_fusion.2
  26.5 3.5 %fusion.32 = (f32[4,384]{1,0:T(4,128)}, f32[4,384,512]{2,1,0:T(8,128)}) fusion(pred[384,512]{1,0:T(8,128)(4,1)S(1)} %broadcast_compare_fusion, bf16[384,4,80]{0,2,1:T(8,128)(2,1)S(1)} %bitcast.66, bf16[512,4,80]{0,2,1:T(8,128)(2,1)S(1)} %bitcast.62), kind=kOutput, calls=%fused_computation.62 | convolution fusion | flops 128975360 | bytes 3921920 | tf_op jit(solution)/shard_map/sub | solution.py:46
  30.1 2.2 fusion.11
  32.3 0.0 copy-done.9
  32.3 0.0 copy-start.14
  32.3 0.4 fusion.34
  32.7 1.3 multiply_reduce_fusion
  34.0 0.1 copy-done.4
  34.2 1.0 multiply_convert_fusion
  35.2 1.3 convolution_convert_fusion.1
  36.5 0.4 fusion.33
  36.9 0.1 fusion.10
  37.0 0.8 fusion.30
  37.8 1.9 collective-permute-start.3
  39.7 3.1 collective-permute-start.2
  42.8 0.3 fusion.12
  43.1 3.3 collective-permute-done.2
  46.3 0.8 fusion.20
  47.1 2.2 scatter-add.6
  49.3 0.0 collective-permute-done.3
  49.3 1.7 slice_add_fusion
  51.0 1.9 scatter-add.9
  52.9 0.1 convert_element_type.74
  53.0 0.8 copy-done.2
  53.7 3.1 fusion.1
  56.9 0.0 all-reduce.7.cloned.1.call-update
  56.9 0.2 all-reduce.9.cloned.1.call-start
  57.1 3.2 convolution_bitcast_fusion.1
  60.4 4.5 %fusion.18 = f32[1280,3,320]{2,0,1:T(8,128)} fusion(bf16[384,2,320]{0,2,1:T(8,128)(2,1)S(1)} %copy-done.3, bf16[384,1,320]{0,2,1:T(8,128)(2,1)S(1)} %bitcast.61, f32[1280]{0:T(1024)S(1)} %copy-done.13, bf16[384,1280]{1,0:T(8,128)(2,1)S(1)} %copy-done.1, f32[384]{0:T(512)S(1)} %copy-done.12), kind=kOutput, calls=%fused_computation.44 | convolution fusion | flops 947159040 | bytes 6642176 | tf_op jit(solution)/shard_map/rd,rcj->dcj/dot_general | solution.py:103
  64.9 0.0 all-reduce.9.cloned.1.call-update
  64.9 0.6 copy-done.15
  65.6 0.6 dynamic-slice.16
  66.8 46.9 %all-reduce.7.cloned.1.call-done = bf16[384,1280]{1,0:T(8,128)(2,1)} async-done(((bf16[384,1280]{1,0:T(8,128)(2,1)}), bf16[384,1280]{1,0:T(8,128)(2,1)}) %all-reduce.7.cloned.1.call-update) | async-done | bytes 983056 | tf_op jit(solution)/shard_map/psum | solution.py:95
  113.7 1.9 fusion.6
  115.6 0.1 dynamic_slice.15
  115.7 1.6 fusion.16
  117.3 0.9 copy.14
  118.2 127.3 %psum.15 = f32[320]{0:T(512)} all-reduce(f32[320]{0:T(512)S(1)} %dynamic_slice.15), channel_id=1, replica_groups=mesh['vis'=64,'head'=4] {'vis'}, use_global_device_ids=true, to_apply=%region_9.10 | all-reduce | flops 320 | bytes 2560 | tf_op jit(solution)/shard_map/psum | solution.py:102
  245.5 77.0 %all-reduce.9.cloned.1.call-done = (f32[1280,3,320]{2,0,1:T(8,128)}, f32[1280,320]{0,1:T(8,128)}) async-done(((f32[1280,3,320]{2,0,1:T(8,128)}, f32[1280,320]{0,1:T(8,128)}), (f32[1280,3,320]{2,0,1:T(8,128)}, f32[1280,320]{0,1:T(8,128)})) %all-reduce.9.cloned.1.call-update) | async-done | bytes 6553616
  322.5 1.6 constant_dynamic-slice_fusion.1
  324.0 1.1 constant_dynamic-slice_fusion
  325.1 0.7 copy.15
  (22 shorter events, 0.1 us)
Async XLA Ops:
  7.2 2.0 copy-start
  7.2 106.5 %all-reduce.7.cloned.1.call-start = ((), (), s32[]{:S(2)}) async-start(), calls=%async_computation | async-start | bytes 1966080 | tf_op jit(solution)/shard_map/psum | solution.py:95
  9.2 2.9 copy-start.11
  9.2 11.6 %copy-start.10 = (s32[24576]{0:T(1024)S(1)}, s32[24576]{0:T(1024)}, u32[]{:S(2)}) copy-start(s32[24576]{0:T(1024)} %param.15) | copy-start | bytes 294916
  9.2 11.8 %copy-start.6 = (bf16[384,1280]{1,0:T(8,128)(2,1)S(1)}, bf16[384,1280]{1,0:T(8,128)(2,1)}, u32[]{:S(2)}) copy-start(bf16[384,1280]{1,0:T(8,128)(2,1)} %param.14) | copy-start | bytes 2949124
  12.0 0.9 copy-start.7
  13.7 10.1 %collective-permute-start = (bf16[64,2,320]{0,2,1:T(8,128)(2,1)}, bf16[64,2,320]{0,2,1:T(8,128)(2,1)}, u32[]{:S(2)}, u32[]{:S(2)}) collective-permute-start(bf16[64,2,320]{0,2,1:T(8,128)(2,1)} %get-tuple-element.42), channel_id=1, source_target_pairs={{0,4},{4,8},{8,12},{12,16},{16,20},{20,24},{24,28},{28,32},{32,36}... | collective-permute-start | bytes 245768 | tf_op jit(solution)/shard_map/ppermute | solution.py:18
  18.2 7.0 %collective-permute-start.1 = (bf16[64,2,320]{0,2,1:T(8,128)(2,1)}, bf16[64,2,320]{0,2,1:T(8,128)(2,1)}, u32[]{:S(2)}, u32[]{:S(2)}) collective-permute-start(bf16[64,2,320]{0,2,1:T(8,128)(2,1)} %get-tuple-element.43), channel_id=1, source_target_pairs={{4,0},{8,4},{12,8},{16,12},{20,16},{24,20},{28,24},{32,28},{36,32}... | collective-permute-start | bytes 245768 | tf_op jit(solution)/shard_map/ppermute | solution.py:21
  20.8 2.9 copy-start.8
  30.1 2.2 copy-start.9
  32.3 1.9 copy-start.4
  32.3 1.9 copy-start.14
  37.8 11.5 %collective-permute-start.3 = (bf16[64,2,320]{0,2,1:T(8,128)(2,1)}, bf16[64,2,320]{0,2,1:T(8,128)(2,1)}, u32[]{:S(2)}, u32[]{:S(2)}) collective-permute-start(bf16[64,2,320]{0,2,1:T(8,128)(2,1)} %get-tuple-element.44), channel_id=1, source_target_pairs={{0,4},{4,8},{8,12},{12,16},{16,20},{20,24},{24,28},{28,32},{32,36}... | collective-permute-start | bytes 245768 | tf_op jit(solution)/shard_map/ppermute | solution.py:29
  39.7 6.6 %collective-permute-start.2 = (bf16[64,2,320]{0,2,1:T(8,128)(2,1)S(1)}, bf16[64,2,320]{0,2,1:T(8,128)(2,1)S(1)}, u32[]{:S(2)}, u32[]{:S(2)}) collective-permute-start(bf16[64,2,320]{0,2,1:T(8,128)(2,1)S(1)} %get-tuple-element.45), channel_id=1, source_target_pairs={{4,0},{8,4},{12,8},{16,12},{20,16},{24,20},{28,24},{32,28},{36,32}... | collective-permute-start | bytes 245768 | tf_op jit(solution)/shard_map/ppermute | solution.py:29
  53.0 0.8 copy-start.2
  56.9 3.5 %copy-start.1 = (bf16[384,1280]{1,0:T(8,128)(2,1)S(1)}, bf16[384,1280]{1,0:T(8,128)(2,1)}, u32[]{:S(2)}) copy-start(bf16[384,1280]{1,0:T(8,128)(2,1)} %param.10) | copy-start | bytes 2949124
  56.9 3.5 %copy-start.12 = (f32[384]{0:T(512)S(1)}, f32[384]{0:T(512)}, u32[]{:S(2)}) copy-start(f32[384]{0:T(512)} %copy-done.11) | copy-start | bytes 4612
  56.9 3.5 %copy-start.13 = (f32[1280]{0:T(1024)S(1)}, f32[1280]{0:T(1024)}, u32[]{:S(2)}) copy-start(f32[1280]{0:T(1024)} %param.11) | copy-start | bytes 15364
  56.9 265.6 %all-reduce.9.cloned.1.call-start = ((), (), s32[]{:S(2)}) async-start(), calls=%async_computation.1 | async-start | bytes 15073280
  57.1 3.3 copy-start.3
  57.1 3.3 copy-start.5
  64.9 0.7 copy-start.15
Sparse Core Ops, SparseCore 0:
  57.0 56.6 all-reduce.6
  117.9 204.5 all-reduce.8
where the time goes:
time: 334 us; the launch traced here: 333 us
  waiting for transfers between devices  129 us (39%)
  blocking collectives  127 us (38%)
  matrix products  24.1 us (7%)
  between operations  15 us (4%)
  local copies, waits for them, and re-layouts  13.6 us (4%)
  starting transfers between devices  12.3 us (4%)
  other arithmetic  11.8 us (4%)
    psum x1, blocking collectives, per_device(): grad_gain = lax.psum(gain_part, 'vis')  127 us
    unnamed x3, waiting for transfers between devices  77 us
    psum x1, waiting for transfers between devices, per_device(): lax.psum(partial_normed.astype(jnp.bfloat16), 'head').astype(jnp.float32)  46.9 us
    unnamed x37, local copies, waits for them, and re-layouts  7.59 us
  transfers between devices with their start and end apart: 6, of which 4 were waited for; matrix products, arithmetic and copies ran while one was open for 6% of the time, Pallas kernels for 0%

commit v1 on v0

v1 whole, which is shorter than its diff:
```python
import functools

import jax
import jax.numpy as jnp
from jax import lax
from jax.experimental import pallas as pl
from jax.experimental.pallas import tpu as pltpu
from jax.sharding import PartitionSpec as P

f32 = jnp.float32
bf16 = jnp.bfloat16
D = 1280
HD = 80
R = 384
SCALE = HD ** (-0.5)
EPS = 1e-06
MESH = pl.DeviceIdType.MESH
NEG = -1e30
WIDTHS = (256, 384)


def nn(a, b):
    return lax.dot_general(a, b, (((1,), (0,)), ((), ())), preferred_element_type=f32)


def nt(a, b, precision=None):
    return lax.dot_general(
        a, b, (((1,), (1,)), ((), ())), preferred_element_type=f32, precision=precision
    )


NAMES = ["proj", "halo0", "halo1", "nt", "gyt", "gt0", "gt1", "core", "gcore"]
NAMES += [f"r{s}{t}" for s in range(2) for t in range(4)]
NAMES += [f"l{s}{t}" for s in range(2) for t in range(4)]
NAMES += [f"x{s}{d}" for s in range(2) for d in range(1, 4)]
NAMES += [f"y{d}" for d in range(1, 4)] + [f"s{d}" for d in range(1, 4)]
NAMES += [f"gx{d}" for d in range(1, 4)] + [f"gz{d}" for d in range(1, 8)]
MSG = {name: i for i, name in enumerate(NAMES)}


def kernel(
    x_hbm, gy_hbm, wt_hbm, wo_hbm, ids_hbm, gain_hbm,
    gx_out, gqkv_out, gout_out, ggain_out,
    x_v, gy_v, wt, wo, ids, gain,
    xt, nrm, gyt, wn, gcol, inv,
    psend, proj, halo, kn, vn, idr, idc, main, sec,
    gt, at, gtr,
    p0, p1, r0, r1, l0, l1, r0h, r1h, l0h, l1h,
    a0, a1, xs0, xs1, xr0, xr1, csend, crecv,
    gnf, ysend, yrecv, ssend, srecv,
    gxs, gxr, gcs, gcr, gzs, gzr,
    lsem, send_sem, recv_sem,
):
    v = lax.axis_index("vis")
    h = lax.axis_index("head")
    c = lax.rem(v, 2)
    q = v // 2
    x = lax.rem(q, 4)
    z = v // 8
    dev = lambda zz, xx, cc: (zz * 8 + xx * 2 + cc, h)
    zdev = lambda d: dev(lax.rem(z + d + 8, 8), x, c)
    xdev = lambda d: dev(z, lax.rem(x + d, 4), c)
    ydev = lambda d: (v, lax.rem(h + d, 4))
    peer = (v + 1 - 2 * c, h)
    chip = lambda d, cc: (2 * lax.rem(q + d + 32, 32) + cc, h)

    loads = []

    def load(src, dst):
        cp = pltpu.make_async_copy(src, dst, lsem.at[len(loads)])
        cp.start()
        loads.append(cp)
        return cp

    ld_x = load(x_hbm, x_v)
    ld_gain = load(gain_hbm, gain)
    ld_gy = load(gy_hbm, gy_v)
    ld_w = []
    for k in (2, 3, 0, 1):
        half = c if k < 2 else 1 - c
        for comp in range(3):
            src = pl.multiple_of(320 * comp + 160 * half + 80 * (k % 2), 16)
            ld_w.append(load(wt_hbm.at[pl.ds(src, 80), :], wt.at[pl.ds(240 * k + 80 * comp, 80), :]))
    for k in (1, 0):
        half = c if k == 0 else 1 - c
        src = pl.multiple_of(160 * half, 16)
        ld_w.append(load(wo_hbm.at[pl.ds(src, 160), :], wo.at[pl.ds(160 * k, 160), :]))
    ld_ids = load(ids_hbm, ids)

    barrier = pltpu.get_barrier_semaphore()
    greet = [peer]
    greet += [zdev(d) for d in range(1, 8)]
    greet += [xdev(d) for d in range(1, 4)]
    greet += [ydev(d) for d in range(1, 4)]
    greet += [chip(2 * c - 1, 0), chip(2 * c - 1, 1), chip(1 - 2 * c, c)]
    for d in greet:
        pl.semaphore_signal(barrier, inc=1, device_id=d, device_id_type=MESH)

    copies = {}

    def send(name, src, dst, to):
        i = MSG[name]
        cp = pltpu.make_async_remote_copy(
            src_ref=src, dst_ref=dst, send_sem=send_sem.at[i], recv_sem=recv_sem.at[i],
            device_id=to, device_id_type=MESH,
        )
        cp.start()
        copies[name] = cp

    def arrived(name):
        copies[name].wait_recv()

    ld_x.wait()
    ld_gain.wait()
    xt[...] = x_v[...].T
    for i in range(10):
        gcol[pl.ds(128 * i, 128), :] = jnp.broadcast_to(gain[pl.ds(i, 1), :], (128, 128)).T
    for b in range(3):
        lanes = pl.ds(128 * b, 128)
        xf = xt[:, lanes].astype(f32)
        iv = lax.rsqrt(jnp.sum(xf * xf, axis=0, keepdims=True) * (1.0 / D) + EPS)
        inv[:, lanes] = iv
        nrm[:, lanes] = (xf * iv * gcol[...]).astype(bf16)
    ld_gy.wait()
    gyt[:, 0:R] = gy_v[...].T
    for cp in ld_w:
        cp.wait()
    ld_ids.wait()

    def project(half, dst):
        pa = nn(wt[pl.ds(480 * half, 480), :], nrm[:, 0:R]).astype(bf16)
        pg = nn(wo[pl.ds(160 * half, 160), :], gyt[:, 0:R]).astype(bf16)
        for b in range(3):
            dst[b, 0:480, :] = pa[:, 128 * b : 128 * b + 128]
            dst[b, 480:640, :] = pg[:, 128 * b : 128 * b + 128]

    project(1, psend)
    pl.semaphore_wait(barrier, len(greet))
    edge = 2 * c
    send("halo1", psend.at[edge], halo.at[c], chip(2 * c - 1, 1 - c))
    send("proj", psend, proj.at[pl.ds(3, 3)], peer)
    project(0, proj)
    send("halo0", proj.at[edge], halo.at[c], chip(2 * c - 1, c))
    send("gyt", gyt.at[:, pl.ds(0, R)], gyt.at[:, pl.ds(R, R)], peer)
    send("nt", nrm.at[:, pl.ds(0, R)], nrm.at[:, pl.ds(R, R)], peer)

    for s in range(3):
        idr[pl.ds(s, 1), :] = ids[pl.ds(6 * q + 3 * c + s, 1), :]
        idr[pl.ds(3 + s, 1), :] = ids[pl.ds(6 * q + 3 - 3 * c + s, 1), :]
    lane1 = lax.broadcasted_iota(jnp.int32, (1, 128), 1) < 64
    after = ids[pl.ds(lax.rem(6 * q + 6, 192), 1), :]
    before = ids[pl.ds(lax.rem(6 * q + 191, 192), 1), :]
    idr[pl.ds(6, 1), :] = jnp.where(lane1, after, before)
    for s in range(7):
        idc[s] = jnp.broadcast_to(idr[pl.ds(s, 1), :], (128, 128)).T

    wn[...] = wt[...].T

    def natural(s):
        for k in range(2):
            kn[2 * s + k] = proj[s, pl.ds(240 * k + 80, 80), :].T
            vn[2 * s + k] = proj[s, pl.ds(240 * k + 160, 80), :].T

    for s in range(3):
        natural(s)
    arrived("proj")
    for s in range(3, 6):
        natural(s)
    arrived("halo0")
    arrived("halo1")
    lane = lax.broadcasted_iota(jnp.int32, (640, 128), 1) < 64
    proj[6] = jnp.where(lane, halo[0].astype(f32), halo[1].astype(f32)).astype(bf16)
    natural(6)

    pick = lambda a, b: jnp.where(c == 0, a, b) if a != b else a
    nxt = [pick(*p) for p in ((1, 1), (2, 2), (3, 6), (4, 4), (5, 5), (6, 0), (0, 3))]
    prv = [pick(*p) for p in ((6, 5), (0, 0), (1, 1), (2, 6), (3, 3), (4, 4), (5, 2))]
    lane80 = lax.broadcasted_iota(jnp.int32, (HD, 128), 1) < 64

    def mixed(a, b):
        return jnp.where(lane80, a.astype(f32), b.astype(f32)).astype(bf16)

    def attend(k, s):
        o = 240 * k
        n, p = nxt[s], prv[s]
        qt = proj[s, pl.ds(o, 80), :]
        gq = proj[s, pl.ds(480 + 80 * k, 80), :]
        kt, vt = [
            jnp.concatenate(
                [
                    proj[s, pl.ds(o + w, 80), :],
                    mixed(proj[n, pl.ds(o + w, 80), :], proj[p, pl.ds(o + w, 80), :]),
                ],
                axis=1,
            )
            for w in (80, 160)
        ]
        kk, vv = [
            jnp.concatenate([t[2 * s + k], t[2 * n + k, 0:64], t[2 * p + k, 64:128]], axis=0)
            for t in (kn, vn)
        ]
        key_ids = jnp.concatenate([idc[s], idc[n, 0:64], idc[p, 64:128]], axis=0)
        same = key_ids == idr[pl.ds(s, 1), :]
        scores = jnp.where(same, nn(kk, qt) * SCALE, NEG)
        e = jnp.exp(scores - jnp.max(scores, axis=0, keepdims=True))
        w = e * (1.0 / jnp.sum(e, axis=0, keepdims=True))
        probs = w.astype(bf16)
        att = nn(vt, probs).astype(bf16)
        delta = jnp.sum(att.astype(f32) * gq.astype(f32), axis=0, keepdims=True)
        ds = (w * (nn(vv, gq) - delta) * SCALE).astype(bf16)
        if s < 6:
            at[pl.ds(80 * k, 80), pl.ds(128 * s, 128)] = att
            gt[pl.ds(o, 80), pl.ds(128 * s, 128)] = nn(kt, ds).astype(bf16)
        gk = nt(qt, ds)
        gv = nt(gq, probs)
        main[s, 0:80, :] = gk[:, 0:128]
        main[s, 80:160, :] = gv[:, 0:128]
        sec[s, 0:80, :] = gk[:, 128:256]
        sec[s, 80:160, :] = gv[:, 128:256]

    lane160 = lax.broadcasted_iota(jnp.int32, (2 * HD, 128), 1) < 64

    def head(k):
        for s in range(7):
            attend(k, s)
        for s in range(6):
            total = main[s] + jnp.where(lane160, sec[prv[s]], sec[nxt[s]])
            gt[pl.ds(240 * k + 80, 160), pl.ds(128 * s, 128)] = total.astype(bf16)
        send(f"gt{k}", gt.at[pl.ds(240 * k, 240), pl.ds(R, R)], gtr.at[pl.ds(240 * k, 240), :], peer)

    part, rr, ll = (p0, p1), ((r0h, r0), (r1h, r1)), ((l0h, l0), (l1h, l1))

    def weights(k):
        a = nt(nrm[...], gt[pl.ds(240 * k, 240), :]).astype(bf16)
        b = nt(gyt[...], at[pl.ds(80 * k, 80), :]).astype(bf16)
        for i in range(8):
            rows = slice(160 * i, 160 * i + 160)
            if k == 0:
                p0[i, :, 0:240] = a[rows]
                p0[i, :, 240:256] = b[rows, 0:16]
                p1[i, :, 0:64] = b[rows, 16:80]
            else:
                p1[i, :, 64:304] = a[rows]
                p1[i, :, 304:384] = b[rows]

    def ring_send(s, t):
        if t == 0:
            far = lax.rem(z + 4, 8)
            send(f"r{s}0", part[s].at[far, pl.ds(0, 80)], rr[s][0], zdev(1))
            send(f"l{s}0", part[s].at[far, pl.ds(80, 80)], ll[s][0], zdev(-1))
        else:
            send(f"r{s}{t}", part[s].at[lax.rem(z + 4 - t, 8)], rr[s][1].at[t - 1], zdev(1))
            send(f"l{s}{t}", part[s].at[lax.rem(z + 4 + t, 8)], ll[s][1].at[t - 1], zdev(-1))

    def ring_add(s, t):
        for way, got, at_ in (("r", rr[s], z + 3 - t), ("l", ll[s], z + 5 + t)):
            arrived(f"{way}{s}{t}")
            i = lax.rem(at_, 8)
            if t == 0:
                rows = pl.ds(0, 80) if way == "r" else pl.ds(80, 80)
                total = part[s][i, rows].astype(f32) + got[0][...].astype(f32)
                part[s][i, rows] = total.astype(bf16)
            else:
                total = part[s][i].astype(f32) + got[1][t - 1].astype(f32)
                part[s][i] = total.astype(bf16)
        ring_send(s, t + 1)

    acc, xs, xr = (a0, a1), (xs0, xs1), (xr0, xr1)

    def ring_end(s):
        arrived(f"r{s}3")
        arrived(f"l{s}3")
        total = part[s][z].astype(f32) + rr[s][1][2].astype(f32) + ll[s][1][2].astype(f32)
        for i in range(4):
            piece = total[40 * i : 40 * i + 40]
            acc[s][i] = piece
            xs[s][i] = jnp.concatenate([piece, jnp.zeros((8, WIDTHS[s]), f32)], axis=0).astype(bf16)
        for d in range(1, 4):
            send(f"x{s}{d}", xs[s].at[lax.rem(x + d, 4)], xr[s].at[d - 1], xdev(d))

    def x_end(s):
        total = acc[s][x]
        for d in range(1, 4):
            arrived(f"x{s}{d}")
            total = total + xr[s][d - 1].astype(f32)[0:40]
        return total

    head(0)
    arrived("gyt")
    arrived("nt")
    weights(0)
    ring_send(0, 0)
    head(1)
    weights(1)
    ring_send(1, 0)
    ring_add(0, 0)

    arrived("gt0")
    arrived("gt1")
    ssum = jnp.zeros((1, R), f32)
    for d in (1, 2, 3, 0):
        to = lax.rem(h + d, 4)
        rows = pl.ds(pl.multiple_of(320 * to, 64), 320)
        g = nn(wn[rows, 0:480], gt[:, 0:R]) + nn(wn[rows, 480:960], gtr[...])
        parts = []
        for b in range(3):
            gb = g[:, 128 * b : 128 * b + 128] * gcol[rows, :]
            xb = xt[rows, pl.ds(128 * b, 128)].astype(f32)
            parts.append(jnp.sum(gb * xb, axis=0, keepdims=True))
        ssum = ssum + jnp.concatenate(parts, axis=1)
        if d:
            ysend[d - 1] = g.astype(bf16)
            send(f"y{d}", ysend.at[d - 1], yrecv.at[d - 1], ydev(d))
        else:
            gnf[...] = g
        if d == 1:
            ring_add(1, 0)
        if d == 3:
            ring_add(0, 1)
    ssend[...] = jnp.broadcast_to(ssum, (8, R))
    for d in range(1, 4):
        send(f"s{d}", ssend, srecv.at[d - 1], ydev(d))
    ring_add(1, 1)
    ring_add(0, 2)
    ring_add(1, 2)
    ring_end(0)

    mine = pl.ds(pl.multiple_of(320 * h, 64), 320)
    gn = gnf[...]
    sums = ssum
    for d in range(1, 4):
        arrived(f"y{d}")
        arrived(f"s{d}")
        gn = gn + yrecv[d - 1].astype(f32)
        sums = sums + srecv[d - 1, 0:1, :]
    iv = inv[...]
    xo = xt[mine, :].astype(f32)
    gc = jnp.concatenate([gcol[mine, :]] * 3, axis=1)
    xi = xo * iv
    gx = gyt[mine, 0:R].astype(f32) + iv * (gn * gc - xi * (iv * (sums * (1.0 / D))))
    gx_out[...] = gx.astype(bf16)
    gxs[...] = nt(jnp.ones((8, R), f32), gn * xi, precision=lax.Precision.HIGHEST)
    for d in range(1, 4):
        send(f"gx{d}", gxs, gxr.at[d - 1], xdev(d))

    ring_end(1)
    total = gxs[...]
    for d in range(1, 4):
        arrived(f"gx{d}")
        total = total + gxr[d - 1]
    gcs[...] = total
    send("gcore", gcs, gcr, peer)
    f0 = x_end(0)
    arrived("gcore")
    gzs[...] = gcs[...] + gcr[...]
    for d in range(1, 8):
        send(f"gz{d}", gzs, gzr.at[d - 1], zdev(d))
    f1 = x_end(1)

    both = jnp.concatenate([f0, f1], axis=1)
    low, high = both[0:20], both[20:40]
    first = c == 0
    csend[0:20, :] = jnp.where(first, high, low)
    csend[20:24, :] = jnp.zeros((4, 640), f32)
    send("core", csend, crecv, peer)
    own = jnp.where(first, low, high)
    total = gzs[...]
    for d in range(1, 8):
        arrived(f"gz{d}")
        total = total + gzr[d - 1]
    ggain_out[...] = total[0:1]
    arrived("core")
    other = crecv[0:20, :]
    sides = (jnp.where(first, own, other), jnp.where(first, other, own))
    for i, side in enumerate(sides):
        for k in range(2):
            col = 80 * (2 * i + k)
            for comp in range(3):
                gqkv_out[comp, :, col : col + 80] = side[:, 320 * k + 80 * comp : 320 * k + 80 * comp + 80]
            gout_out[:, col : col + 80] = side[:, 320 * k + 240 : 320 * k + 320]
    for cp in copies.values():
        cp.wait_send()


def per_device(patches, norm_gain, w_qkv, w_out, grad_y, window_ids):
    wt = jnp.transpose(w_qkv, (1, 2, 0)).reshape(960, D)
    wo = jnp.transpose(w_out)
    V = pltpu.VMEM
    w0, w1 = WIDTHS
    scratch = [
        V((R, D), bf16), V((R, D), bf16), V((960, D), bf16), V((320, D), bf16),
        V((192, 128), jnp.int32), V((10, 128), f32),
        V((D, R), bf16), V((D, 2 * R), bf16), V((D, 2 * R), bf16), V((D, 960), bf16),
        V((D, 128), f32), V((1, R), f32),
        V((3, 640, 128), bf16), V((7, 640, 128), bf16), V((2, 640, 128), bf16),
        V((14, 128, HD), bf16), V((14, 128, HD), bf16),
        V((8, 128), jnp.int32), V((7, 128, 128), jnp.int32),
        V((7, 160, 128), f32), V((7, 160, 128), f32),
        V((480, 2 * R), bf16), V((160, 2 * R), bf16), V((480, R), bf16),
        V((8, 160, w0), bf16), V((8, 160, w1), bf16),
        V((3, 160, w0), bf16), V((3, 160, w1), bf16),
        V((3, 160, w0), bf16), V((3, 160, w1), bf16),
        V((80, w0), bf16), V((80, w1), bf16), V((80, w0), bf16), V((80, w1), bf16),
        V((4, 40, w0), f32), V((4, 40, w1), f32),
        V((4, 48, w0), bf16), V((4, 48, w1), bf16),
        V((3, 48, w0), bf16), V((3, 48, w1), bf16),
        V((24, 640), f32), V((24, 640), f32),
        V((320, R), f32), V((3, 320, R), bf16), V((3, 320, R), bf16),
        V((8, R), f32), V((3, 8, R), f32),
        V((8, 320), f32), V((3, 8, 320), f32), V((8, 320), f32), V((8, 320), f32),
        V((8, 320), f32), V((7, 8, 320), f32),
        pltpu.SemaphoreType.DMA((18,)),
        pltpu.SemaphoreType.DMA((len(NAMES),)),
        pltpu.SemaphoreType.DMA((len(NAMES),)),
    ]
    gx, gqkv, gout, ggain = pl.pallas_call(
        kernel,
        out_shape=(
            jax.ShapeDtypeStruct((320, R), bf16),
            jax.ShapeDtypeStruct((3, 20, 320), f32),
            jax.ShapeDtypeStruct((20, 320), f32),
            jax.ShapeDtypeStruct((1, 320), f32),
        ),
        in_specs=[pl.BlockSpec(memory_space=pl.ANY)] * 6,
        out_specs=[pl.BlockSpec(memory_space=pltpu.VMEM)] * 4,
        scratch_shapes=scratch,
        compiler_params=pltpu.CompilerParams(
            collective_id=0, has_side_effects=True, vmem_limit_bytes=56 * 1024 * 1024
        ),
    )(patches, grad_y, wt, wo, window_ids.reshape(192, 128), norm_gain.reshape(10, 128))
    return gx.T, jnp.transpose(gqkv, (1, 0, 2)), gout, ggain.reshape(320)


def solution(mesh):
    in_specs = (P("vis", None), P(), P(None, None, "head"), P(None, "head"), P("vis", None), P())
    out_specs = (P("vis", "head"), P("vis", None, "head"), P("vis", "head"), P("head"))
    return jax.shard_map(
        per_device, mesh=mesh, in_specs=in_specs, out_specs=out_specs, check_vma=False
    )
```

time: 334 us -> 60.8 us (0.18)
  waiting for transfers between devices: 129 us -> 0 us
  blocking collectives: 127 us -> 0 us
  Pallas kernels: 0 us -> 53.6 us
  matrix products: 24.1 us -> 0 us
  between operations: 15 us -> 0.64 us
  starting transfers between devices: 12.3 us -> 0 us
  other arithmetic: 11.8 us -> 1.25 us
  local copies, waits for them, and re-layouts: 13.6 us -> 4.59 us
    psum x1 -> x0, blocking collectives: 127 us -> none  [per_device(): grad_gain = lax.psum(gain_part, 'vis')]
    unnamed x3 -> x0, waiting for transfers between devices: 77 us -> none
    pallas_call x0 -> x1, Pallas kernels: none -> 53.6 us  [per_device(): pl.pallas_call(kernel, out_shape=(jax.ShapeDtypeStruct((320, R), bf16), j...]
    psum x1 -> x0, waiting for transfers between devices: 46.9 us -> none  [per_device(): lax.psum(partial_normed.astype(jnp.bfloat16), 'head').astype(jnp.float32)]
    dot_general x10 -> x0, matrix products: 20.6 us -> none  [the longest x1 4.49 us: per_device(): jnp.einsum('rd,rcj->dcj', normed, grad_proj, preferred_element_type=f32)]
    ppermute x4 -> x0, starting transfers between devices: 12.1 us -> none  [the longest x2 4.97 us: from_behind(): return lax.ppermute(block, axis, route)]
    ppermute x4 -> x0, waiting for transfers between devices: 4.62 us -> none  [the longest x2 3.26 us: from_behind(): return lax.ppermute(block, axis, route)]
    scatter-add x2 -> x0, local copies, waits for them, and re-layouts: 4.08 us -> none  [the longest x1 2.2 us: per_device(): center = center.at[row_count - WIN:].add(from_below)]
  transfers between devices with their start and end apart: 6 -> 0, of which waited for: 4 -> 0; matrix products, arithmetic and copies ran while one was open for 6% -> 0% of each run, Pallas kernels for 0% -> 0%
where the time goes in v1:
time: 60.8 us; the launch traced here: 60.1 us
  Pallas kernels  53.6 us (88%)
  local copies, waits for them, and re-layouts  4.59 us (8%)
  other arithmetic  1.25 us (2%)
  between operations  0.64 us (1%)
    pallas_call x1, Pallas kernels, per_device(): pl.pallas_call(kernel, out_shape=(jax.ShapeDtypeStruct((320, R), bf16), j...  53.6 us
    unnamed x3, local copies, waits for them, and re-layouts  4.59 us
    pallas_call x1, other arithmetic, per_device(): pl.pallas_call(kernel, out_shape=(jax.ShapeDtypeStruct((320, R), bf16), j...  1.25 us

profile of v1, /device:TPU:1, one launch (start us, length us, event | category | flops | bytes accessed | tf_op | source)
XLA Modules:
  0.0 60.1 jit_solution(12713957328564613594)
XLA Ops:
  0.6 53.6 %shard_map.93 = (bf16[320,384]{1,0:T(8,128)(2,1)}, f32[3,20,320]{2,1,0:T(8,128)}, f32[20,320]{1,0:T(8,128)}, f32[1,320]{1,0:T(1,128)}) custom-call(bf16[384,1280]{1,0:T(8,128)(2,1)} %x_hbm.1, bf16[384,1280]{1,0:T(8,128)(2,1)} %gy_hbm.1, bf16[960,1280]{1,0:T(8,128)(2,1)} %bitcast.8, bf16[320,1280]{1,0:T(8,128)(2,1)} %bitcast.9, s32[192,128]{1,0:T(8,128)} %bitcast.12, ...), custom_call_target="tpu_custom_call" | custom-call | tf_op jit(solution)/shard_map/pallas_call | solution.py:416
  54.3 1.2 %reduce = f32[320]{0:T(512)} reduce(f32[1,320]{1,0:T(1,128)} %get-tuple-element.11, f32[]{:T(128)} %constant), dimensions={0}, to_apply=%get-tuple-element.11.reduce_sub_computation | reduce | bytes 2564 | tf_op jit(solution)/shard_map/pallas_call | solution.py:416
  55.5 1.7 %copy.13 = bf16[384,320]{0,1:T(8,128)(2,1)} copy(bf16[384,320]{0,1:T(8,128)(2,1)} %bitcast.10) | data formatting | bytes 491520
  57.2 1.5 %copy.14 = f32[20,3,320]{2,0,1:T(8,128)} copy(f32[20,3,320]{2,0,1:T(8,128)} %bitcast.11) | data formatting | bytes 153600
  58.7 1.4 %copy.15 = f32[20,320]{1,0:T(8,128)} copy(f32[20,320]{1,0:T(8,128)} %get-tuple-element.18) | data formatting | bytes 51200

commit v2 on v1

v2 whole, which is shorter than its diff:
```python
import functools

import jax
import jax.numpy as jnp
from jax import lax
from jax.experimental import pallas as pl
from jax.experimental.pallas import tpu as pltpu
from jax.sharding import PartitionSpec as P

f32 = jnp.float32
bf16 = jnp.bfloat16
D = 1280
HD = 80
R = 384
SCALE = HD ** (-0.5)
EPS = 1e-06
MESH = pl.DeviceIdType.MESH
NEG = -1e30
WZ = 256
WX = 384
TILES = WX // 128
WAYS = {"r": 1, "l": -1}


def hops(way, half):
    return 4 if (way == "r") == (half == 0) else 3


def nn(a, b):
    return lax.dot_general(a, b, (((1,), (0,)), ((), ())), preferred_element_type=f32)


def nt(a, b, precision=None):
    return lax.dot_general(
        a, b, (((1,), (1,)), ((), ())), preferred_element_type=f32, precision=precision
    )


NAMES = ["proj", "halo0", "halo1", "nt", "gyt", "gt", "core", "gcore"]
NAMES += [f"{w}{k}{j}" for w in WAYS for k in range(2) for j in range(hops(w, k))]
NAMES += [f"xs{d}" for d in range(1, 4)]
NAMES += [f"x{t}{d}" for t in range(TILES) for d in range(1, 4)]
NAMES += [f"z{t}{d}" for t in range(TILES) for d in range(1, 8)]
NAMES += [f"{n}{d}" for n in ("y", "s", "gx", "gy") for d in range(1, 4)]
NAMES += [f"gz{d}" for d in range(1, 8)]
MSG = {name: i for i, name in enumerate(NAMES)}


def kernel(
    x_hbm, gy_hbm, wt_hbm, wo_hbm, ids_hbm, gain_hbm,
    gx_out, gqkv_out, gout_out, ggain_out,
    x_v, gy_v, wt, wo, ids, gain,
    xt, nrm, gyt, wn, gcol, inv,
    psend, proj, hsend, halo, kn, vn, idr, idc, main, sec,
    gt, at, gtr,
    pz, ring, acc, xs, xr,
    px, pxr, accx, zs, zr, csend, crecv,
    gnf, ysend, yrecv, ssend, srecv,
    gp, gxr, gcs, gcr, gzs, gzr, gys, gyr,
    lsem, send_sem, recv_sem,
):
    v = lax.axis_index("vis")
    h = lax.axis_index("head")
    c = lax.rem(v, 2)
    q = v // 2
    x = lax.rem(q, 4)
    z = v // 8
    dev = lambda zz, xx, cc: (zz * 8 + xx * 2 + cc, h)
    zdev = lambda d: dev(lax.rem(z + d + 8, 8), x, c)
    xdev = lambda d: dev(z, lax.rem(x + d, 4), c)
    ydev = lambda d: (v, lax.rem(h + d, 4))
    peer = (v + 1 - 2 * c, h)
    chip = lambda d, cc: (2 * lax.rem(q + d + 32, 32) + cc, h)

    loads = []

    def load(src, dst):
        cp = pltpu.make_async_copy(src, dst, lsem.at[len(loads)])
        cp.start()
        loads.append(cp)
        return cp

    ld_x = load(x_hbm, x_v)
    ld_gain = load(gain_hbm, gain)
    ld_gy = load(gy_hbm, gy_v)
    ld_w = []
    for k in (1, 0):
        half = c if k == 0 else 1 - c
        for comp in range(3):
            src = pl.multiple_of(320 * comp + 160 * half, 16)
            ld_w.append(load(wt_hbm.at[pl.ds(src, 160), :], wt.at[pl.ds(480 * k + 160 * comp, 160), :]))
        src = pl.multiple_of(160 * half, 16)
        ld_w.append(load(wo_hbm.at[pl.ds(src, 160), :], wo.at[pl.ds(160 * k, 160), :]))
    ld_ids = load(ids_hbm, ids)

    barrier = pltpu.get_barrier_semaphore()
    greet = [peer]
    greet += [zdev(d) for d in range(1, 8)]
    greet += [xdev(d) for d in range(1, 4)]
    greet += [ydev(d) for d in range(1, 4)]
    greet += [chip(2 * c - 1, 0), chip(2 * c - 1, 1), chip(1 - 2 * c, c)]
    for d in greet:
        pl.semaphore_signal(barrier, inc=1, device_id=d, device_id_type=MESH)

    copies = {}

    def send(name, src, dst, to):
        i = MSG[name]
        cp = pltpu.make_async_remote_copy(
            src_ref=src, dst_ref=dst, send_sem=send_sem.at[i], recv_sem=recv_sem.at[i],
            device_id=to, device_id_type=MESH,
        )
        cp.start()
        copies[name] = cp

    def arrived(name):
        copies[name].wait_recv()
    ld_x.wait()
    ld_gain.wait()
    xt[...] = x_v[...].T
    for i in range(10):
        gcol[pl.ds(128 * i, 128), :] = jnp.broadcast_to(gain[pl.ds(i, 1), :], (128, 128)).T
    for b in range(3):
        lanes = pl.ds(128 * b, 128)
        xf = xt[:, lanes].astype(f32)
        iv = lax.rsqrt(jnp.sum(xf * xf, axis=0, keepdims=True) * (1.0 / D) + EPS)
        inv[:, lanes] = iv
        nrm[:, lanes] = (xf * iv * gcol[...]).astype(bf16)
    ld_gy.wait()
    gyt[:, 0:R] = gy_v[...].T
    for cp in ld_w:
        cp.wait()
    ld_ids.wait()
    def project(half, dst):
        pa = nn(wt[pl.ds(480 * half, 480), :], nrm[:, 0:R]).astype(bf16)
        pg = nn(wo[pl.ds(160 * half, 160), :], gyt[:, 0:R]).astype(bf16)
        for b in range(3):
            dst[b, 0:480, :] = pa[:, 128 * b : 128 * b + 128]
            dst[b, 480:640, :] = pg[:, 128 * b : 128 * b + 128]

    project(1, psend)
    pl.semaphore_wait(barrier, len(greet))
    edge = 2 * c
    lane320 = lax.broadcasted_iota(jnp.int32, (320, 128), 1) < 64

    def pack_halo(k, block):
        top, low = block[0:320].astype(f32), block[320:640].astype(f32)
        first = jnp.where(lane320, top, pltpu.roll(low, 64, 1))
        last = jnp.where(lane320, pltpu.roll(top, 64, 1), low)
        hsend[k] = jnp.where(c == 0, first, last).astype(bf16)

    pack_halo(1, psend[edge])
    send("halo1", hsend.at[1], halo.at[c], chip(2 * c - 1, 1 - c))
    send("proj", psend, proj.at[pl.ds(3, 3)], peer)
    project(0, proj)
    pack_halo(0, proj[edge])
    send("halo0", hsend.at[0], halo.at[c], chip(2 * c - 1, c))
    send("gyt", gyt.at[:, pl.ds(0, R)], gyt.at[:, pl.ds(R, R)], peer)
    send("nt", nrm.at[:, pl.ds(0, R)], nrm.at[:, pl.ds(R, R)], peer)
    for s in range(3):
        idr[pl.ds(s, 1), :] = ids[pl.ds(6 * q + 3 * c + s, 1), :]
        idr[pl.ds(3 + s, 1), :] = ids[pl.ds(6 * q + 3 - 3 * c + s, 1), :]
    lane1 = lax.broadcasted_iota(jnp.int32, (1, 128), 1) < 64
    after = ids[pl.ds(lax.rem(6 * q + 6, 192), 1), :]
    before = ids[pl.ds(lax.rem(6 * q + 191, 192), 1), :]
    idr[pl.ds(6, 1), :] = jnp.where(lane1, after, before)
    for s in range(7):
        idc[s] = jnp.broadcast_to(idr[pl.ds(s, 1), :], (128, 128)).T

    wn[...] = wt[...].T

    def natural(s):
        kn[s] = proj[s, 160:320, :].T
        vn[s] = proj[s, 320:480, :].T

    for s in range(3):
        natural(s)
    arrived("proj")
    for s in range(3, 6):
        natural(s)

    pick = lambda a, b: jnp.where(c == 0, a, b) if a != b else a
    nxt = [pick(*p) for p in ((1, 1), (2, 2), (3, 6), (4, 4), (5, 5), (6, 0), (0, 3))]
    prv = [pick(*p) for p in ((6, 5), (0, 0), (1, 1), (2, 6), (3, 3), (4, 4), (5, 2))]
    lane160 = lax.broadcasted_iota(jnp.int32, (160, 128), 1) < 64
    zero = jnp.zeros((HD, 128), bf16)

    def diagonal(t):
        return jnp.concatenate(
            [jnp.concatenate([t[0:80], zero], axis=1), jnp.concatenate([zero, t[80:160]], axis=1)], axis=0
        )

    def diag_of(t):
        return jnp.concatenate([t[0:80, 0:128], t[80:160, 128:256]], axis=0)

    def attend(s, n, p, inside=True):
        q2, g2 = diagonal(proj[s, 0:160, :]), diagonal(proj[s, 480:640, :])
        kt, vt = [
            jnp.concatenate(
                [
                    proj[s, w : w + 160, :],
                    jnp.where(lane160, proj[n, w : w + 160, :].astype(f32), proj[p, w : w + 160, :].astype(f32)).astype(bf16),
                ],
                axis=1,
            )
            for w in (160, 320)
        ]
        kk, vv = [jnp.concatenate([t[s], t[n, 0:64], t[p, 64:128]], axis=0) for t in (kn, vn)]
        key_ids = jnp.concatenate([idc[s], idc[n, 0:64], idc[p, 64:128]], axis=0)
        same = key_ids == idr[pl.ds(s, 1), :]
        same = jnp.concatenate([same, same], axis=1)
        scores = jnp.where(same, nn(kk, q2) * SCALE, NEG)
        e = jnp.exp(scores - jnp.max(scores, axis=0, keepdims=True))
        w = e * (1.0 / jnp.sum(e, axis=0, keepdims=True))
        probs = w.astype(bf16)
        att = diag_of(nn(vt, probs)).astype(bf16)
        both = att.astype(f32) * proj[s, 480:640, :].astype(f32)
        delta = jnp.concatenate(
            [jnp.sum(both[0:80], axis=0, keepdims=True), jnp.sum(both[80:160], axis=0, keepdims=True)], axis=1
        )
        ds = (w * (nn(vv, g2) - delta) * SCALE).astype(bf16)
        if inside:
            lanes = pl.ds(pl.multiple_of(128 * s, 128), 128)
            at[:, lanes] = att
            gt[0:160, lanes] = diag_of(nn(kt, ds)).astype(bf16)
        gk = nt(q2, ds)
        gv = nt(g2, probs)
        main[s, 0:160, :] = gk[:, 0:128]
        main[s, 160:320, :] = gv[:, 0:128]
        sec[s, 0:160, :] = gk[:, 128:256]
        sec[s, 160:320, :] = gv[:, 128:256]

    attend(1, 2, 0)
    attend(pick(2, 0), pick(3, 1), pick(1, 5))
    attend(pick(3, 5), pick(4, 0), pick(2, 4))
    attend(4, 5, 3)

    arrived("halo0")
    arrived("halo1")
    ha, hb = halo[0].astype(f32), halo[1].astype(f32)
    proj[6, 0:320, :] = jnp.where(lane320, ha, pltpu.roll(hb, 64, 1)).astype(bf16)
    proj[6, 320:640, :] = jnp.where(lane320, pltpu.roll(ha, 64, 1), hb).astype(bf16)
    natural(6)
    attend(pick(0, 2), pick(1, 6), pick(6, 1))
    attend(pick(5, 3), pick(6, 4), pick(4, 6))
    attend(6, nxt[6], prv[6], inside=False)
    lane320 = lax.broadcasted_iota(jnp.int32, (320, 128), 1) < 64
    for s in (3, 4, 5, 0, 1, 2):
        total = main[s] + jnp.where(lane320, sec[prv[s]], sec[nxt[s]])
        gt[160:480, 128 * s : 128 * s + 128] = total.astype(bf16)
        if s == 5:
            send("gt", gt.at[:, pl.ds(R, R)], gtr, peer)

    def ring_send(way, k, j):
        n = hops(way, k)
        chunk = lax.rem(z + 8 + WAYS[way] * (n - j), 8)
        slot = ring.at[4 * (2 * (way == "l") + k) + j]
        send(f"{way}{k}{j}", pz.at[chunk, pl.ds(80 * k, 80)], slot, zdev(WAYS[way]))

    def ring_add(j):
        for k in range(2):
            for way in WAYS:
                n = hops(way, k)
                if j < n - 1:
                    arrived(f"{way}{k}{j}")
                    chunk = lax.rem(z + 8 + WAYS[way] * (n - 1 - j), 8)
                    rows = pl.ds(80 * k, 80)
                    got = ring[4 * (2 * (way == "l") + k) + j]
                    pz[chunk, rows] = (pz[chunk, rows].astype(f32) + got.astype(f32)).astype(bf16)
                    ring_send(way, k, j + 1)

    def ring_end():
        for k in range(2):
            total = pz[z, pl.ds(80 * k, 80)].astype(f32)
            for way in WAYS:
                j = hops(way, k) - 1
                arrived(f"{way}{k}{j}")
                total = total + ring[4 * (2 * (way == "l") + k) + j].astype(f32)
            for i in range(2):
                piece = total[40 * i : 40 * i + 40]
                acc[2 * k + i] = piece
                xs[2 * k + i] = jnp.concatenate([piece, jnp.zeros((8, WZ), f32)], axis=0).astype(bf16)
        for d in (2, 1, 3):
            send(f"xs{d}", xs.at[lax.rem(x + d, 4)], xr.at[d - 1], xdev(d))

    def x_sum(t):
        total = px[t, x].astype(f32)
        for d in range(1, 4):
            arrived(f"x{t}{d}")
            total = total + pxr[t, d - 1].astype(f32)
        for i in range(8):
            piece = total[40 * i : 40 * i + 40]
            accx[t, i] = piece
            zs[t, i] = jnp.concatenate([piece, jnp.zeros((8, 128), f32)], axis=0).astype(bf16)
        for d in (4, 3, 5, 2, 6, 1, 7):
            send(f"z{t}{d}", zs.at[t, lax.rem(z + d, 8)], zr.at[t, d - 1], zdev(d))

    def z_sum(t):
        total = accx[t, z]
        for d in range(1, 8):
            arrived(f"z{t}{d}")
            total = total + zr[t, d - 1].astype(f32)[0:40]
        return total

    arrived("gyt")
    arrived("nt")
    first_z = nt(nrm[...], gt[0:WZ, :]).astype(bf16)
    for i in range(8):
        pz[i] = first_z[160 * i : 160 * i + 160]
    for k in range(2):
        for way in WAYS:
            ring_send(way, k, 0)
    first_x = jnp.concatenate([nt(nrm[...], gt[WZ:480, :]), nt(gyt[...], at[...])], axis=1)
    for i in range(4):
        rows = [first_x[160 * j + 40 * i : 160 * j + 40 * i + 40] for j in range(8)]
        rows = jnp.concatenate(rows, axis=0).astype(bf16)
        for t in range(TILES):
            px[t, i] = rows[:, 128 * t : 128 * t + 128]
    for t in range(TILES):
        for d in (2, 1, 3):
            send(f"x{t}{d}", px.at[t, lax.rem(x + d, 4)], pxr.at[t, d - 1], xdev(d))

    arrived("gt")
    ssum = jnp.zeros((1, R), f32)
    gp[...] = jnp.zeros((8, 320), f32)
    ones = jnp.ones((8, 128), bf16)
    for d in (2, 1, 3, 0):
        to = lax.rem(h + d, 4)
        rows = pl.ds(pl.multiple_of(320 * to, 64), 320)
        g = nn(wn[rows, 0:480], gt[:, 0:R]) + nn(wn[rows, 480:960], gtr[...])
        if d:
            ysend[d - 1] = g.astype(bf16)
            send(f"y{d}", ysend.at[d - 1], yrecv.at[d - 1], ydev(d))
        else:
            gnf[...] = g
        parts = []
        gains = jnp.zeros((320, 128), f32)
        for b in range(3):
            lanes = slice(128 * b, 128 * b + 128)
            gb = g[:, lanes] * xt[rows, lanes].astype(f32)
            parts.append(jnp.sum(gb * gcol[rows, :], axis=0, keepdims=True))
            gains = gains + gb * inv[:, lanes]
        ssum = ssum + jnp.concatenate(parts, axis=1)
        high = gains.astype(bf16)
        low = (gains - high.astype(f32)).astype(bf16)
        gp[pl.ds(to, 1), :] = (nt(ones, high) + nt(ones, low))[0:1]
    ssend[...] = jnp.broadcast_to(ssum, (8, R))
    for d in range(1, 4):
        send(f"s{d}", ssend, srecv.at[d - 1], ydev(d))
    for d in range(1, 4):
        send(f"gx{d}", gp, gxr.at[d - 1], xdev(d))
    ring_add(0)
    x_sum(0)
    ring_add(1)
    total = gp[...]
    for d in range(1, 4):
        arrived(f"gx{d}")
        total = total + gxr[d - 1]
    gcs[...] = total
    send("gcore", gcs, gcr, peer)
    x_sum(1)
    ring_add(2)
    arrived("gcore")
    gzs[...] = gcs[...] + gcr[...]
    for d in range(1, 8):
        send(f"gz{d}", gzs, gzr.at[d - 1], zdev(d))
    x_sum(2)
    ring_end()

    mine = pl.ds(pl.multiple_of(320 * h, 64), 320)
    gn = gnf[...]
    sums = ssum
    for d in range(1, 4):
        arrived(f"y{d}")
        arrived(f"s{d}")
        gn = gn + yrecv[d - 1].astype(f32)
        sums = sums + srecv[d - 1, 0:1, :]
    iv = inv[...]
    gc = jnp.concatenate([gcol[mine, :]] * 3, axis=1)
    xi = xt[mine, :].astype(f32) * iv
    gx = gyt[mine, 0:R].astype(f32) + iv * (gn * gc - xi * (iv * (sums * (1.0 / D))))
    gx_out[...] = gx.astype(bf16)

    total = gzs[...]
    for d in range(1, 8):
        arrived(f"gz{d}")
        total = total + gzr[d - 1]
    gys[...] = total
    for d in range(1, 4):
        send(f"gy{d}", gys, gyr.at[d - 1], ydev(d))

    parts = [None] + [z_sum(t) for t in range(TILES)]
    total = acc[x]
    for d in range(1, 4):
        arrived(f"xs{d}")
        total = total + xr[d - 1].astype(f32)[0:40]
    parts[0] = total
    both = jnp.concatenate(parts, axis=1)
    low, high = both[0:20], both[20:40]
    first = c == 0
    csend[0:20, :] = jnp.where(first, high, low)
    csend[20:24, :] = jnp.zeros((4, 640), f32)
    send("core", csend, crecv, peer)
    own = jnp.where(first, low, high)
    total = gys[pl.ds(h, 1), :]
    for d in range(1, 4):
        arrived(f"gy{d}")
        total = total + gyr[d - 1, pl.ds(h, 1), :]
    ggain_out[...] = total[0]
    arrived("core")
    other = crecv[0:20, :]
    sides = (jnp.where(first, own, other), jnp.where(first, other, own))
    for i, side in enumerate(sides):
        cols = slice(160 * i, 160 * i + 160)
        for comp in range(3):
            gqkv_out[comp, :, cols] = side[:, 160 * comp : 160 * comp + 160]
        gout_out[:, cols] = side[:, 480:640]
    for cp in copies.values():
        cp.wait_send()


def hand_over(*refs):
    for src, dst in zip(refs[:4], refs[4:]):
        dst[...] = src[...]


def per_device(patches, norm_gain, w_qkv, w_out, grad_y, window_ids):
    wt = jnp.transpose(w_qkv, (1, 2, 0)).reshape(960, D)
    wo = jnp.transpose(w_out)
    V = pltpu.VMEM
    scratch = [
        V((R, D), bf16), V((R, D), bf16), V((960, D), bf16), V((320, D), bf16),
        V((192, 128), jnp.int32), V((10, 128), f32),
        V((D, R), bf16), V((D, 2 * R), bf16), V((D, 2 * R), bf16), V((D, 960), bf16),
        V((D, 128), f32), V((1, R), f32),
        V((3, 640, 128), bf16), V((7, 640, 128), bf16), V((2, 320, 128), bf16), V((2, 320, 128), bf16),
        V((7, 128, 160), bf16), V((7, 128, 160), bf16),
        V((8, 128), jnp.int32), V((7, 128, 128), jnp.int32),
        V((7, 320, 128), f32), V((7, 320, 128), f32),
        V((480, 2 * R), bf16), V((160, 2 * R), bf16), V((480, R), bf16),
        V((8, 160, WZ), bf16), V((16, 80, WZ), bf16),
        V((4, 40, WZ), f32), V((4, 48, WZ), bf16), V((3, 48, WZ), bf16),
        V((TILES, 4, 320, 128), bf16), V((TILES, 3, 320, 128), bf16),
        V((TILES, 8, 40, 128), f32), V((TILES, 8, 48, 128), bf16), V((TILES, 7, 48, 128), bf16),
        V((24, 640), f32), V((24, 640), f32),
        V((320, R), f32), V((3, 320, R), bf16), V((3, 320, R), bf16),
        V((8, R), f32), V((3, 8, R), f32),
        V((8, 320), f32), V((3, 8, 320), f32), V((8, 320), f32), V((8, 320), f32),
        V((8, 320), f32), V((7, 8, 320), f32), V((8, 320), f32), V((3, 8, 320), f32),
        pltpu.SemaphoreType.DMA((12,)),
        pltpu.SemaphoreType.DMA((len(NAMES),)),
        pltpu.SemaphoreType.DMA((len(NAMES),)),
    ]
    results = pl.pallas_call(
        kernel,
        out_shape=(
            jax.ShapeDtypeStruct((320, R), bf16),
            jax.ShapeDtypeStruct((3, 20, 320), f32),
            jax.ShapeDtypeStruct((20, 320), f32),
            jax.ShapeDtypeStruct((320,), f32),
        ),
        in_specs=[pl.BlockSpec(memory_space=pl.ANY)] * 6,
        out_specs=[pl.BlockSpec(memory_space=pltpu.VMEM)] * 4,
        scratch_shapes=scratch,
        compiler_params=pltpu.CompilerParams(
            collective_id=0, has_side_effects=True, vmem_limit_bytes=56 * 1024 * 1024
        ),
    )(patches, grad_y, wt, wo, window_ids.reshape(192, 128), norm_gain.reshape(10, 128))
    vmem = pl.BlockSpec(memory_space=pltpu.VMEM)
    gx, gqkv, gout, ggain = pl.pallas_call(
        hand_over,
        out_shape=tuple(jax.ShapeDtypeStruct(r.shape, r.dtype) for r in results),
        in_specs=[vmem] * 4,
        out_specs=[vmem] * 4,
    )(*results)
    return gx.T, jnp.transpose(gqkv, (1, 0, 2)), gout, ggain


def solution(mesh):
    in_specs = (P("vis", None), P(), P(None, None, "head"), P(None, "head"), P("vis", None), P())
    out_specs = (P("vis", "head"), P("vis", None, "head"), P("vis", "head"), P("head"))
    return jax.shard_map(
        per_device, mesh=mesh, in_specs=in_specs, out_specs=out_specs, check_vma=False
    )
```

time: 60.8 us -> 50.8 us (0.84)
  the two profiles are of different devices: /device:TPU:1 before, /device:TPU:2 now
where the time goes in v2:
time: 50.8 us; the launch traced here: 50.7 us
  Pallas kernels  50.1 us (99%)
  between operations  0.64 us (1%)
    pallas_call x1, Pallas kernels, per_device(): pl.pallas_call(kernel, out_shape=(jax.ShapeDtypeStruct((320, R), bf16), j...  48.3 us
    pallas_call x1, Pallas kernels, per_device(): pl.pallas_call(hand_over, out_shape=tuple((jax.ShapeDtypeStruct(r.shape,...  1.75 us

profile of v2, /device:TPU:2, one launch (start us, length us, event | category | flops | bytes accessed | tf_op | source)
XLA Modules:
  0.0 50.7 jit_solution(8599583972865865606)
XLA Ops:
  0.6 48.3 %shard_map.93 = (bf16[320,384]{1,0:T(8,128)(2,1)}, f32[3,20,320]{2,1,0:T(8,128)}, f32[20,320]{1,0:T(8,128)}, f32[320]{0:T(512)}) custom-call(bf16[384,1280]{1,0:T(8,128)(2,1)} %x_hbm.1, bf16[384,1280]{1,0:T(8,128)(2,1)} %gy_hbm.1, bf16[960,1280]{1,0:T(8,128)(2,1)} %bitcast.8, bf16[320,1280]{1,0:T(8,128)(2,1)} %bitcast.9, s32[192,128]{1,0:T(8,128)} %bitcast.10, ...), custom_call_target="tpu_custom_call" | custom-call | tf_op jit(solution)/shard_map/pallas_call | solution.py:454
  49.0 1.7 %shard_map.94 = (bf16[320,384]{1,0:T(8,128)(2,1)}, f32[3,20,320]{2,1,0:T(8,128)}, f32[20,320]{1,0:T(8,128)}, f32[320]{0:T(512)}) custom-call(bf16[320,384]{1,0:T(8,128)(2,1)} %get-tuple-element.12.refs_0_, f32[3,20,320]{2,1,0:T(8,128)} %get-tuple-element.13.refs_1_, f32[20,320]{1,0:T(8,128)} %get-tuple-element.14.refs_2_, f32[320]{0:T(512)} %get-tuple-element.15.refs_3_), custom_call_target="tpu_custom_call" | custom-call | tf_op jit(solution)/shard_map/pallas_call | solution.py:470

commit v3 on v2

--- a/solution.py
+++ b/solution.py
@@ -19,11 +19,7 @@
 WZ = 256
 WX = 384
 TILES = WX // 128
-WAYS = {"r": 1, "l": -1}
-
-
-def hops(way, half):
-    return 4 if (way == "r") == (half == 0) else 3
+WAYS = (1, -1)
 
 
 def nn(a, b):
@@ -37,9 +33,9 @@
 
 
 NAMES = ["proj", "halo0", "halo1", "nt", "gyt", "gt", "core", "gcore"]
-NAMES += [f"{w}{k}{j}" for w in WAYS for k in range(2) for j in range(hops(w, k))]
+NAMES += [f"z{n}{w}" for n in "ahnb" for w in range(2)]
 NAMES += [f"xs{d}" for d in range(1, 4)]
-NAMES += [f"x{t}{d}" for t in range(TILES) for d in range(1, 4)]
+NAMES += [f"x{n}{t}{w}" for n in "ab" for t in range(TILES) for w in range(2)]
 NAMES += [f"z{t}{d}" for t in range(TILES) for d in range(1, 8)]
 NAMES += [f"{n}{d}" for n in ("y", "s", "gx", "gy") for d in range(1, 4)]
 NAMES += [f"gz{d}" for d in range(1, 8)]
@@ -53,8 +49,8 @@
     xt, nrm, gyt, wn, gcol, inv,
     psend, proj, hsend, halo, kn, vn, idr, idc, main, sec,
     gt, at, gtr,
-    pz, ring, acc, xs, xr,
-    px, pxr, accx, zs, zr, csend, crecv,
+    pz, za, zh, zn, zb, acc, xs, xr,
+    px, xa, xb, accx, zs, zr, csend, crecv,
     gnf, ysend, yrecv, ssend, srecv,
     gp, gxr, gcs, gcr, gzs, gzr, gys, gyr,
     lsem, send_sem, recv_sem,
@@ -67,7 +63,7 @@
     z = v // 8
     dev = lambda zz, xx, cc: (zz * 8 + xx * 2 + cc, h)
     zdev = lambda d: dev(lax.rem(z + d + 8, 8), x, c)
-    xdev = lambda d: dev(z, lax.rem(x + d, 4), c)
+    xdev = lambda d: dev(z, lax.rem(x + d + 4, 4), c)
     ydev = lambda d: (v, lax.rem(h + d, 4))
     peer = (v + 1 - 2 * c, h)
     chip = lambda d, cc: (2 * lax.rem(q + d + 32, 32) + cc, h)
@@ -251,43 +247,55 @@
         if s == 5:
             send("gt", gt.at[:, pl.ds(R, R)], gtr, peer)
 
-    def ring_send(way, k, j):
-        n = hops(way, k)
-        chunk = lax.rem(z + 8 + WAYS[way] * (n - j), 8)
-        slot = ring.at[4 * (2 * (way == "l") + k) + j]
-        send(f"{way}{k}{j}", pz.at[chunk, pl.ds(80 * k, 80)], slot, zdev(WAYS[way]))
-
-    def ring_add(j):
-        for k in range(2):
-            for way in WAYS:
-                n = hops(way, k)
-                if j < n - 1:
-                    arrived(f"{way}{k}{j}")
-                    chunk = lax.rem(z + 8 + WAYS[way] * (n - 1 - j), 8)
-                    rows = pl.ds(80 * k, 80)
-                    got = ring[4 * (2 * (way == "l") + k) + j]
-                    pz[chunk, rows] = (pz[chunk, rows].astype(f32) + got.astype(f32)).astype(bf16)
-                    ring_send(way, k, j + 1)
-
-    def ring_end():
-        for k in range(2):
-            total = pz[z, pl.ds(80 * k, 80)].astype(f32)
-            for way in WAYS:
-                j = hops(way, k) - 1
-                arrived(f"{way}{k}{j}")
-                total = total + ring[4 * (2 * (way == "l") + k) + j].astype(f32)
-            for i in range(2):
-                piece = total[40 * i : 40 * i + 40]
-                acc[2 * k + i] = piece
-                xs[2 * k + i] = jnp.concatenate([piece, jnp.zeros((8, WZ), f32)], axis=0).astype(bf16)
+    def z_start():
+        for w, way in enumerate(WAYS):
+            send(f"za{w}", pz.at[lax.rem(z + 8 + 3 * way, 8)], za.at[w], zdev(way))
+        for w, way in enumerate(WAYS):
+            send(f"zh{w}", pz.at[lax.rem(z + 4, 8), pl.ds(80 * w, 80)], zh.at[w], zdev(2 * way))
+        for w, way in enumerate(WAYS):
+            send(f"zn{w}", pz.at[lax.rem(z + 8 + way, 8)], zn.at[w], zdev(way))
+
+    def z_pass():
+        for w, way in enumerate(WAYS):
+            arrived(f"za{w}")
+            arrived(f"zh{w}")
+            chunk = lax.rem(z + 8 + 2 * way, 8)
+            for k in range(2):
+                rows = pl.ds(80 * k, 80)
+                total = pz[chunk, rows].astype(f32) + za[w, rows].astype(f32)
+                if k == w:
+                    total = total + zh[w].astype(f32)
+                pz[chunk, rows] = total.astype(bf16)
+            send(f"zb{w}", pz.at[chunk], zb.at[w], zdev(2 * way))
+
+    def z_end():
+        total = pz[z].astype(f32)
+        for w in range(2):
+            arrived(f"zn{w}")
+            arrived(f"zb{w}")
+            total = total + zn[w].astype(f32) + zb[w].astype(f32)
+        for i in range(4):
+            piece = total[40 * i : 40 * i + 40]
+            acc[i] = piece
+            xs[i] = jnp.concatenate([piece, jnp.zeros((8, WZ), f32)], axis=0).astype(bf16)
         for d in (2, 1, 3):
             send(f"xs{d}", xs.at[lax.rem(x + d, 4)], xr.at[d - 1], xdev(d))
 
+    def x_start(t):
+        for w, way in enumerate(WAYS):
+            send(f"xa{t}{w}", px.at[t, lax.rem(x + 2, 4), pl.ds(160 * w, 160)], xa.at[t, w], xdev(way))
+
+    def x_pass(t):
+        for w, way in enumerate(WAYS):
+            arrived(f"xa{t}{w}")
+            chunk, rows = lax.rem(x + 4 + way, 4), pl.ds(160 * w, 160)
+            px[t, chunk, rows] = (px[t, chunk, rows].astype(f32) + xa[t, w].astype(f32)).astype(bf16)
+            send(f"xb{t}{w}", px.at[t, chunk], xb.at[t, w], xdev(way))
+
     def x_sum(t):
-        total = px[t, x].astype(f32)
-        for d in range(1, 4):
-            arrived(f"x{t}{d}")
-            total = total + pxr[t, d - 1].astype(f32)
+        arrived(f"xb{t}0")
+        arrived(f"xb{t}1")
+        total = px[t, x].astype(f32) + xb[t, 0].astype(f32) + xb[t, 1].astype(f32)
         for i in range(8):
             piece = total[40 * i : 40 * i + 40]
             accx[t, i] = piece
@@ -307,9 +315,7 @@
     first_z = nt(nrm[...], gt[0:WZ, :]).astype(bf16)
     for i in range(8):
         pz[i] = first_z[160 * i : 160 * i + 160]
-    for k in range(2):
-        for way in WAYS:
-            ring_send(way, k, 0)
+    z_start()
     first_x = jnp.concatenate([nt(nrm[...], gt[WZ:480, :]), nt(gyt[...], at[...])], axis=1)
     for i in range(4):
         rows = [first_x[160 * j + 40 * i : 160 * j + 40 * i + 40] for j in range(8)]
@@ -317,8 +323,7 @@
         for t in range(TILES):
             px[t, i] = rows[:, 128 * t : 128 * t + 128]
     for t in range(TILES):
-        for d in (2, 1, 3):
-            send(f"x{t}{d}", px.at[t, lax.rem(x + d, 4)], pxr.at[t, d - 1], xdev(d))
+        x_start(t)
 
     arrived("gt")
     ssum = jnp.zeros((1, R), f32)
@@ -349,23 +354,29 @@
         send(f"s{d}", ssend, srecv.at[d - 1], ydev(d))
     for d in range(1, 4):
         send(f"gx{d}", gp, gxr.at[d - 1], xdev(d))
-    ring_add(0)
-    x_sum(0)
-    ring_add(1)
+    for t in range(TILES):
+        x_pass(t)
     total = gp[...]
     for d in range(1, 4):
         arrived(f"gx{d}")
         total = total + gxr[d - 1]
     gcs[...] = total
     send("gcore", gcs, gcr, peer)
-    x_sum(1)
-    ring_add(2)
+    z_pass()
     arrived("gcore")
     gzs[...] = gcs[...] + gcr[...]
+    for d in (4, 3, 5, 2, 6, 1, 7):
+        send(f"gz{d}", gzs, gzr.at[d - 1], zdev(d))
+    for t in range(TILES):
+        x_sum(t)
+    total = gzs[...]
     for d in range(1, 8):
-        send(f"gz{d}", gzs, gzr.at[d - 1], zdev(d))
-    x_sum(2)
-    ring_end()
+        arrived(f"gz{d}")
+        total = total + gzr[d - 1]
+    gys[...] = total
+    for d in range(1, 4):
+        send(f"gy{d}", gys, gyr.at[d - 1], ydev(d))
+    z_end()
 
     mine = pl.ds(pl.multiple_of(320 * h, 64), 320)
     gn = gnf[...]
@@ -380,14 +391,6 @@
     xi = xt[mine, :].astype(f32) * iv
     gx = gyt[mine, 0:R].astype(f32) + iv * (gn * gc - xi * (iv * (sums * (1.0 / D))))
     gx_out[...] = gx.astype(bf16)
-
-    total = gzs[...]
-    for d in range(1, 8):
-        arrived(f"gz{d}")
-        total = total + gzr[d - 1]
-    gys[...] = total
-    for d in range(1, 4):
-        send(f"gy{d}", gys, gyr.at[d - 1], ydev(d))
 
     parts = [None] + [z_sum(t) for t in range(TILES)]
     total = acc[x]
@@ -438,9 +441,11 @@
         V((8, 128), jnp.int32), V((7, 128, 128), jnp.int32),
         V((7, 320, 128), f32), V((7, 320, 128), f32),
         V((480, 2 * R), bf16), V((160, 2 * R), bf16), V((480, R), bf16),
-        V((8, 160, WZ), bf16), V((16, 80, WZ), bf16),
+        V((8, 160, WZ), bf16), V((2, 160, WZ), bf16), V((2, 80, WZ), bf16),
+        V((2, 160, WZ), bf16), V((2, 160, WZ), bf16),
         V((4, 40, WZ), f32), V((4, 48, WZ), bf16), V((3, 48, WZ), bf16),
-        V((TILES, 4, 320, 128), bf16), V((TILES, 3, 320, 128), bf16),
+        V((TILES, 4, 320, 128), bf16), V((TILES, 2, 160, 128), bf16),
+        V((TILES, 2, 320, 128), bf16),
         V((TILES, 8, 40, 128), f32), V((TILES, 8, 48, 128), bf16), V((TILES, 7, 48, 128), bf16),
         V((24, 640), f32), V((24, 640), f32),
         V((320, R), f32), V((3, 320, R), bf16), V((3, 320, R), bf16),

time: 50.8 us -> 47.9 us (0.943)
  the two profiles are of different devices: /device:TPU:2 before, /device:TPU:1 now
where the time goes in v3:
time: 47.9 us; the launch traced here: 47.8 us
  Pallas kernels  47.1 us (98%)
  between operations  0.64 us (1%)
    pallas_call x1, Pallas kernels, per_device(): pl.pallas_call(kernel, out_shape=(jax.ShapeDtypeStruct((320, R), bf16), j...  45.4 us
    pallas_call x1, Pallas kernels, per_device(): pl.pallas_call(hand_over, out_shape=tuple((jax.ShapeDtypeStruct(r.shape,...  1.75 us

profile of v3, /device:TPU:1, one launch (start us, length us, event | category | flops | bytes accessed | tf_op | source)
XLA Modules:
  0.0 47.8 jit_solution(10592370366526078347)
XLA Ops:
  0.6 45.4 %shard_map.93 = (bf16[320,384]{1,0:T(8,128)(2,1)}, f32[3,20,320]{2,1,0:T(8,128)}, f32[20,320]{1,0:T(8,128)}, f32[320]{0:T(512)}) custom-call(bf16[384,1280]{1,0:T(8,128)(2,1)} %x_hbm.1, bf16[384,1280]{1,0:T(8,128)(2,1)} %gy_hbm.1, bf16[960,1280]{1,0:T(8,128)(2,1)} %bitcast.8, bf16[320,1280]{1,0:T(8,128)(2,1)} %bitcast.9, s32[192,128]{1,0:T(8,128)} %bitcast.10, ...), custom_call_target="tpu_custom_call" | custom-call | tf_op jit(solution)/shard_map/pallas_call | solution.py:459
  46.0 1.7 %shard_map.94 = (bf16[320,384]{1,0:T(8,128)(2,1)}, f32[3,20,320]{2,1,0:T(8,128)}, f32[20,320]{1,0:T(8,128)}, f32[320]{0:T(512)}) custom-call(bf16[320,384]{1,0:T(8,128)(2,1)} %get-tuple-element.12.refs_0_, f32[3,20,320]{2,1,0:T(8,128)} %get-tuple-element.13.refs_1_, f32[20,320]{1,0:T(8,128)} %get-tuple-element.14.refs_2_, f32[320]{0:T(512)} %get-tuple-element.15.refs_3_), custom_call_target="tpu_custom_call" | custom-call | tf_op jit(solution)/shard_map/pallas_call | solution.py:475

commit v4 on v3

--- a/solution.py
+++ b/solution.py
@@ -16,8 +16,8 @@
 EPS = 1e-06
 MESH = pl.DeviceIdType.MESH
 NEG = -1e30
-WZ = 256
-WX = 384
+WZ = 128
+WX = 512
 TILES = WX // 128
 WAYS = (1, -1)
 
@@ -47,7 +47,7 @@
     gx_out, gqkv_out, gout_out, ggain_out,
     x_v, gy_v, wt, wo, ids, gain,
     xt, nrm, gyt, wn, gcol, inv,
-    psend, proj, hsend, halo, kn, vn, idr, idc, main, sec,
+    psend, proj, hsend, halo, kn, vn, idr, idc, main, sec, wts, delta,
     gt, at, gtr,
     pz, za, zh, zn, zb, acc, xs, xr,
     px, xa, xb, accx, zs, zr, csend, crecv,
@@ -189,47 +189,56 @@
     def diag_of(t):
         return jnp.concatenate([t[0:80, 0:128], t[80:160, 128:256]], axis=0)
 
-    def attend(s, n, p, inside=True):
+    def lanes_of(s):
+        return pl.ds(pl.multiple_of(128 * s, 128), 128)
+
+    def keys_t(s, n, p, w):
+        rest = jnp.where(lane160, proj[n, w : w + 160, :].astype(f32), proj[p, w : w + 160, :].astype(f32))
+        return jnp.concatenate([proj[s, w : w + 160, :], rest.astype(bf16)], axis=1)
+
+    def keys_n(t, s, n, p):
+        return jnp.concatenate([t[s], t[n, 0:64], t[p, 64:128]], axis=0)
+
+    def forward(s, n, p, inside=True):
         q2, g2 = diagonal(proj[s, 0:160, :]), diagonal(proj[s, 480:640, :])
-        kt, vt = [
-            jnp.concatenate(
-                [
-                    proj[s, w : w + 160, :],
-                    jnp.where(lane160, proj[n, w : w + 160, :].astype(f32), proj[p, w : w + 160, :].astype(f32)).astype(bf16),
-                ],
-                axis=1,
-            )
-            for w in (160, 320)
-        ]
-        kk, vv = [jnp.concatenate([t[s], t[n, 0:64], t[p, 64:128]], axis=0) for t in (kn, vn)]
-        key_ids = jnp.concatenate([idc[s], idc[n, 0:64], idc[p, 64:128]], axis=0)
-        same = key_ids == idr[pl.ds(s, 1), :]
+        same = keys_n(idc, s, n, p) == idr[pl.ds(s, 1), :]
         same = jnp.concatenate([same, same], axis=1)
-        scores = jnp.where(same, nn(kk, q2) * SCALE, NEG)
+        scores = jnp.where(same, nn(keys_n(kn, s, n, p), q2) * SCALE, NEG)
         e = jnp.exp(scores - jnp.max(scores, axis=0, keepdims=True))
         w = e * (1.0 / jnp.sum(e, axis=0, keepdims=True))
+        wts[s] = w
         probs = w.astype(bf16)
-        att = diag_of(nn(vt, probs)).astype(bf16)
+        att = diag_of(nn(keys_t(s, n, p, 320), probs)).astype(bf16)
         both = att.astype(f32) * proj[s, 480:640, :].astype(f32)
-        delta = jnp.concatenate(
+        delta[pl.ds(s, 1), :] = jnp.concatenate(
             [jnp.sum(both[0:80], axis=0, keepdims=True), jnp.sum(both[80:160], axis=0, keepdims=True)], axis=1
         )
-        ds = (w * (nn(vv, g2) - delta) * SCALE).astype(bf16)
         if inside:
-            lanes = pl.ds(pl.multiple_of(128 * s, 128), 128)
-            at[:, lanes] = att
-            gt[0:160, lanes] = diag_of(nn(kt, ds)).astype(bf16)
+            at[:, lanes_of(s)] = att
+        gv = nt(g2, probs)
+        main[s, 160:320, :] = gv[:, 0:128]
+        sec[s, 160:320, :] = gv[:, 128:256]
+
+    def backward(s, n, p, inside=True):
+        q2, g2 = diagonal(proj[s, 0:160, :]), diagonal(proj[s, 480:640, :])
+        ds = (wts[s] * (nn(keys_n(vn, s, n, p), g2) - delta[pl.ds(s, 1), :]) * SCALE).astype(bf16)
+        if inside:
+            gt[0:160, lanes_of(s)] = diag_of(nn(keys_t(s, n, p, 160), ds)).astype(bf16)
         gk = nt(q2, ds)
-        gv = nt(g2, probs)
         main[s, 0:160, :] = gk[:, 0:128]
-        main[s, 160:320, :] = gv[:, 0:128]
         sec[s, 0:160, :] = gk[:, 128:256]
-        sec[s, 160:320, :] = gv[:, 128:256]
-
-    attend(1, 2, 0)
-    attend(pick(2, 0), pick(3, 1), pick(1, 5))
-    attend(pick(3, 5), pick(4, 0), pick(2, 4))
-    attend(4, 5, 3)
+
+    def combine(rows, to):
+        for s in range(6):
+            total = main[s, rows, :] + jnp.where(lane160, sec[prv[s], rows, :], sec[nxt[s], rows, :])
+            gt[to : to + 160, 128 * s : 128 * s + 128] = total.astype(bf16)
+
+    inner = [(1, 2, 0), (pick(2, 0), pick(3, 1), pick(1, 5)), (pick(3, 5), pick(4, 0), pick(2, 4)), (4, 5, 3)]
+    outer = [(pick(0, 2), pick(1, 6), pick(6, 1)), (pick(5, 3), pick(6, 4), pick(4, 6)), (6, nxt[6], prv[6], False)]
+    for block in inner:
+        forward(*block)
+    for block in inner:
+        backward(*block)
 
     arrived("halo0")
     arrived("halo1")
@@ -237,15 +246,9 @@
     proj[6, 0:320, :] = jnp.where(lane320, ha, pltpu.roll(hb, 64, 1)).astype(bf16)
     proj[6, 320:640, :] = jnp.where(lane320, pltpu.roll(ha, 64, 1), hb).astype(bf16)
     natural(6)
-    attend(pick(0, 2), pick(1, 6), pick(6, 1))
-    attend(pick(5, 3), pick(6, 4), pick(4, 6))
-    attend(6, nxt[6], prv[6], inside=False)
-    lane320 = lax.broadcasted_iota(jnp.int32, (320, 128), 1) < 64
-    for s in (3, 4, 5, 0, 1, 2):
-        total = main[s] + jnp.where(lane320, sec[prv[s]], sec[nxt[s]])
-        gt[160:480, 128 * s : 128 * s + 128] = total.astype(bf16)
-        if s == 5:
-            send("gt", gt.at[:, pl.ds(R, R)], gtr, peer)
+    for block in outer:
+        forward(*block)
+    combine(slice(160, 320), 320)
 
     def z_start():
         for w, way in enumerate(WAYS):
@@ -312,22 +315,38 @@
 
     arrived("gyt")
     arrived("nt")
+    cols = jnp.concatenate([nt(gyt[...], at[...]), nt(nrm[...], gt[320:480, :])], axis=1)
+
+    def by_owner(cols, i):
+        rows = [cols[160 * j + 40 * i : 160 * j + 40 * i + 40] for j in range(8)]
+        return jnp.concatenate(rows, axis=0).astype(bf16)
+
+    for i in range(4):
+        rows = by_owner(cols, i)
+        px[0, i] = rows[:, 0:128]
+        px[1, i] = rows[:, 128:256]
+        px[2, i, :, 0:64] = rows[:, 256:320]
+    x_start(0)
+    x_start(1)
+
+    for block in outer:
+        backward(*block)
+    combine(slice(0, 160), 160)
+    send("gt", gt.at[:, pl.ds(R, R)], gtr, peer)
     first_z = nt(nrm[...], gt[0:WZ, :]).astype(bf16)
     for i in range(8):
         pz[i] = first_z[160 * i : 160 * i + 160]
     z_start()
-    first_x = jnp.concatenate([nt(nrm[...], gt[WZ:480, :]), nt(gyt[...], at[...])], axis=1)
+    cols = nt(nrm[...], gt[WZ:320, :])
     for i in range(4):
-        rows = [first_x[160 * j + 40 * i : 160 * j + 40 * i + 40] for j in range(8)]
-        rows = jnp.concatenate(rows, axis=0).astype(bf16)
-        for t in range(TILES):
-            px[t, i] = rows[:, 128 * t : 128 * t + 128]
-    for t in range(TILES):
-        x_start(t)
+        rows = by_owner(cols, i)
+        px[2, i, :, 64:128] = rows[:, 0:64]
+        px[3, i] = rows[:, 64:192]
+    x_start(2)
+    x_start(3)
 
     arrived("gt")
     ssum = jnp.zeros((1, R), f32)
-    gp[...] = jnp.zeros((8, 320), f32)
     ones = jnp.ones((8, 128), bf16)
     for d in (2, 1, 3, 0):
         to = lax.rem(h + d, 4)
@@ -338,6 +357,10 @@
             send(f"y{d}", ysend.at[d - 1], yrecv.at[d - 1], ydev(d))
         else:
             gnf[...] = g
+        if d == 1:
+            x_pass(0)
+        if d == 3:
+            x_pass(1)
         parts = []
         gains = jnp.zeros((320, 128), f32)
         for b in range(3):
@@ -352,31 +375,33 @@
     ssend[...] = jnp.broadcast_to(ssum, (8, R))
     for d in range(1, 4):
         send(f"s{d}", ssend, srecv.at[d - 1], ydev(d))
-    for d in range(1, 4):
-        send(f"gx{d}", gp, gxr.at[d - 1], xdev(d))
-    for t in range(TILES):
-        x_pass(t)
+    for d in (4, 3, 5, 2, 6, 1, 7):
+        send(f"gz{d}", gp, gzr.at[d - 1], zdev(d))
+    x_pass(2)
+    x_pass(3)
+    z_pass()
+    x_sum(0)
+    x_sum(1)
     total = gp[...]
+    for d in range(1, 8):
+        arrived(f"gz{d}")
+        total = total + gzr[d - 1]
+    gzs[...] = total
+    for d in range(1, 4):
+        send(f"gx{d}", gzs, gxr.at[d - 1], xdev(d))
+    x_sum(2)
+    x_sum(3)
+    total = gzs[...]
     for d in range(1, 4):
         arrived(f"gx{d}")
         total = total + gxr[d - 1]
     gcs[...] = total
     send("gcore", gcs, gcr, peer)
-    z_pass()
+    z_end()
     arrived("gcore")
-    gzs[...] = gcs[...] + gcr[...]
-    for d in (4, 3, 5, 2, 6, 1, 7):
-        send(f"gz{d}", gzs, gzr.at[d - 1], zdev(d))
-    for t in range(TILES):
-        x_sum(t)
-    total = gzs[...]
-    for d in range(1, 8):
-        arrived(f"gz{d}")
-        total = total + gzr[d - 1]
-    gys[...] = total
+    gys[...] = gcs[...] + gcr[...]
     for d in range(1, 4):
         send(f"gy{d}", gys, gyr.at[d - 1], ydev(d))
-    z_end()
 
     mine = pl.ds(pl.multiple_of(320 * h, 64), 320)
     gn = gnf[...]
@@ -415,9 +440,10 @@
     sides = (jnp.where(first, own, other), jnp.where(first, other, own))
     for i, side in enumerate(sides):
         cols = slice(160 * i, 160 * i + 160)
-        for comp in range(3):
-            gqkv_out[comp, :, cols] = side[:, 160 * comp : 160 * comp + 160]
-        gout_out[:, cols] = side[:, 480:640]
+        gqkv_out[0, :, cols] = jnp.concatenate([side[:, 0:128], side[:, 448:480]], axis=1)
+        gqkv_out[1, :, cols] = side[:, 480:640]
+        gqkv_out[2, :, cols] = side[:, 288:448]
+        gout_out[:, cols] = side[:, 128:288]
     for cp in copies.values():
         cp.wait_send()
 
@@ -440,6 +466,7 @@
         V((7, 128, 160), bf16), V((7, 128, 160), bf16),
         V((8, 128), jnp.int32), V((7, 128, 128), jnp.int32),
         V((7, 320, 128), f32), V((7, 320, 128), f32),
+        V((7, 256, 256), f32), V((8, 256), f32),
         V((480, 2 * R), bf16), V((160, 2 * R), bf16), V((480, R), bf16),
         V((8, 160, WZ), bf16), V((2, 160, WZ), bf16), V((2, 80, WZ), bf16),
         V((2, 160, WZ), bf16), V((2, 160, WZ), bf16),
@@ -450,8 +477,8 @@
         V((24, 640), f32), V((24, 640), f32),
         V((320, R), f32), V((3, 320, R), bf16), V((3, 320, R), bf16),
         V((8, R), f32), V((3, 8, R), f32),
-        V((8, 320), f32), V((3, 8, 320), f32), V((8, 320), f32), V((8, 320), f32),
-        V((8, 320), f32), V((7, 8, 320), f32), V((8, 320), f32), V((3, 8, 320), f32),
+        V((4, 320), f32), V((3, 4, 320), f32), V((4, 320), f32), V((4, 320), f32),
+        V((4, 320), f32), V((7, 4, 320), f32), V((4, 320), f32), V((3, 4, 320), f32),
         pltpu.SemaphoreType.DMA((12,)),
         pltpu.SemaphoreType.DMA((len(NAMES),)),
         pltpu.SemaphoreType.DMA((len(NAMES),)),

time: 47.9 us -> 44.8 us (0.935)
  Pallas kernels: 47.1 us -> 44 us
    pallas_call x1, Pallas kernels: 45.4 us -> 42.3 us  [per_device(): pl.pallas_call(kernel, out_shape=(jax.ShapeDtypeStruct((320, R), bf16), j...]
where the time goes in v4:
time: 44.8 us; the launch traced here: 44.7 us
  Pallas kernels  44 us (98%)
  between operations  0.64 us (1%)
    pallas_call x1, Pallas kernels, per_device(): pl.pallas_call(kernel, out_shape=(jax.ShapeDtypeStruct((320, R), bf16), j...  42.3 us
    pallas_call x1, Pallas kernels, per_device(): pl.pallas_call(hand_over, out_shape=tuple((jax.ShapeDtypeStruct(r.shape,...  1.75 us

profile of v4, /device:TPU:1, one launch (start us, length us, event | category | flops | bytes accessed | tf_op | source)
XLA Modules:
  0.0 44.7 jit_solution(6898975280370513157)
XLA Ops:
  0.6 42.3 %shard_map.93 = (bf16[320,384]{1,0:T(8,128)(2,1)}, f32[3,20,320]{2,1,0:T(8,128)}, f32[20,320]{1,0:T(8,128)}, f32[320]{0:T(512)}) custom-call(bf16[384,1280]{1,0:T(8,128)(2,1)} %x_hbm.1, bf16[384,1280]{1,0:T(8,128)(2,1)} %gy_hbm.1, bf16[960,1280]{1,0:T(8,128)(2,1)} %bitcast.8, bf16[320,1280]{1,0:T(8,128)(2,1)} %bitcast.9, s32[192,128]{1,0:T(8,128)} %bitcast.10, ...), custom_call_target="tpu_custom_call" | custom-call | tf_op jit(solution)/shard_map/pallas_call | solution.py:486
  42.9 1.7 %shard_map.94 = (bf16[320,384]{1,0:T(8,128)(2,1)}, f32[3,20,320]{2,1,0:T(8,128)}, f32[20,320]{1,0:T(8,128)}, f32[320]{0:T(512)}) custom-call(bf16[320,384]{1,0:T(8,128)(2,1)} %get-tuple-element.12.refs_0_, f32[3,20,320]{2,1,0:T(8,128)} %get-tuple-element.13.refs_1_, f32[20,320]{1,0:T(8,128)} %get-tuple-element.14.refs_2_, f32[320]{0:T(512)} %get-tuple-element.15.refs_3_), custom_call_target="tpu_custom_call" | custom-call | tf_op jit(solution)/shard_map/pallas_call | solution.py:502

commit v5 on v4

--- a/solution.py
+++ b/solution.py
@@ -378,8 +378,8 @@
     for d in (4, 3, 5, 2, 6, 1, 7):
         send(f"gz{d}", gp, gzr.at[d - 1], zdev(d))
     x_pass(2)
+    z_pass()
     x_pass(3)
-    z_pass()
     x_sum(0)
     x_sum(1)
     total = gp[...]
@@ -390,6 +390,7 @@
     for d in range(1, 4):
         send(f"gx{d}", gzs, gxr.at[d - 1], xdev(d))
     x_sum(2)
+    z_end()
     x_sum(3)
     total = gzs[...]
     for d in range(1, 4):
@@ -397,7 +398,6 @@
         total = total + gxr[d - 1]
     gcs[...] = total
     send("gcore", gcs, gcr, peer)
-    z_end()
     arrived("gcore")
     gys[...] = gcs[...] + gcr[...]
     for d in range(1, 4):

time: 44.8 us -> 44.6 us (level)
  no operation moved by 1% of the time
where the time goes in v5:
time: 44.6 us; the launch traced here: 44.5 us
  Pallas kernels  43.9 us (98%)
  between operations  0.64 us (1%)
    pallas_call x1, Pallas kernels, per_device(): pl.pallas_call(kernel, out_shape=(jax.ShapeDtypeStruct((320, R), bf16), j...  42.1 us
    pallas_call x1, Pallas kernels, per_device(): pl.pallas_call(hand_over, out_shape=tuple((jax.ShapeDtypeStruct(r.shape,...  1.75 us

profile of v5, /device:TPU:1, one launch (start us, length us, event | category | flops | bytes accessed | tf_op | source)
XLA Modules:
  0.0 44.5 jit_solution(17110743856774431324)
XLA Ops:
  0.6 42.1 %shard_map.93 = (bf16[320,384]{1,0:T(8,128)(2,1)}, f32[3,20,320]{2,1,0:T(8,128)}, f32[20,320]{1,0:T(8,128)}, f32[320]{0:T(512)}) custom-call(bf16[384,1280]{1,0:T(8,128)(2,1)} %x_hbm.1, bf16[384,1280]{1,0:T(8,128)(2,1)} %gy_hbm.1, bf16[960,1280]{1,0:T(8,128)(2,1)} %bitcast.8, bf16[320,1280]{1,0:T(8,128)(2,1)} %bitcast.9, s32[192,128]{1,0:T(8,128)} %bitcast.10, ...), custom_call_target="tpu_custom_call" | custom-call | tf_op jit(solution)/shard_map/pallas_call | solution.py:486
  42.8 1.7 %shard_map.94 = (bf16[320,384]{1,0:T(8,128)(2,1)}, f32[3,20,320]{2,1,0:T(8,128)}, f32[20,320]{1,0:T(8,128)}, f32[320]{0:T(512)}) custom-call(bf16[320,384]{1,0:T(8,128)(2,1)} %get-tuple-element.12.refs_0_, f32[3,20,320]{2,1,0:T(8,128)} %get-tuple-element.13.refs_1_, f32[20,320]{1,0:T(8,128)} %get-tuple-element.14.refs_2_, f32[320]{0:T(512)} %get-tuple-element.15.refs_3_), custom_call_target="tpu_custom_call" | custom-call | tf_op jit(solution)/shard_map/pallas_call | solution.py:502
